TPU v7x, 128 devices: a whole 4x4x4 slice. The times are simulated.
128 devices in a mesh: mom: 16 (over x, z_lo, core), tm: 8 (over z_hi, y).
Axes of the slice: x: 4, y: 4, z: 4 (z_hi: 2, z_lo: 2; z = z_hi * 2 + z_lo), core: 2. Of those that a mesh axis runs over, the one named last changes fastest.
Arguments:
- lesser: float32 [2, 256, 2, 2, 256, 256], P(None, 'mom', None, None, 'tm'), may hold values from -6 to 6
- greater: float32 [2, 256, 2, 2, 256, 256], P(None, 'mom', None, None, 'tm'), may hold values from -6 to 6
- site_of: int32 [256], replicated, may hold values from 0 to 255, as said below
Outputs:
- polarization: float32 [2, 256, 2, 2, 256, 256], P(None, 'mom', None, None, 'tm')
Inputs may be any that keep to these rules, and one draw needn't show every extreme that they name: `site_of`: each of 0 to 255 appears once.
All inputs are finite; a program needn't handle non-finite values.
Results may differ from a plain program's by a relative error of at most 0.0003.
Values sent between devices are 32-bit elements; how exact they have to be, the bound alone decides.
No kernel may reach another device: no remote copies, remote signals or barrier semaphores. Data moves between devices by JAX's collectives and lax.ppermute only.
A program may use at most 128 MiB of HBM per device.

v0:
```python
import math

import jax
import jax.numpy as jnp
from jax import lax
from jax.sharding import PartitionSpec as P

L = 16


def phase_tables(site_of):
    momenta = site_of.shape[0]
    lattice = jnp.arange(momenta, dtype=jnp.int32)
    turn_count = (
        (lattice // L)[:, None] * (site_of // L)[None, :]
        + (lattice % L)[:, None] * (site_of % L)[None, :]
    ) % L
    angles = turn_count.astype(jnp.float32) * (2.0 * math.pi / L)
    scaling = 1.0 / math.sqrt(momenta)
    cosine = jnp.cos(angles) * scaling
    sine_part = jnp.sin(angles) * scaling
    forward = jnp.concatenate(
        [jnp.concatenate([cosine, -sine_part], 1), jnp.concatenate([sine_part, cosine], 1)], 0
    )
    mirrored = jnp.concatenate(
        [jnp.concatenate([cosine, sine_part], 1), jnp.concatenate([-sine_part, cosine], 1)], 0
    )
    backward = jnp.concatenate(
        [jnp.concatenate([cosine.T, sine_part.T], 1), jnp.concatenate([-sine_part.T, cosine.T], 1)],
        0,
    )
    return (forward, mirrored, backward)


def transform(matrix, values):
    dims_in = values.shape
    flattened = values.reshape(dims_in[0] * dims_in[1], -1)
    return jnp.dot(matrix, flattened, precision=lax.Precision.HIGHEST).reshape(dims_in)


def swap_times(values):
    narrow = values.shape[5]
    identity = jnp.eye(narrow, dtype=jnp.float32)
    return jnp.einsum("ckabtu,su->ckbast", values, identity, precision=lax.Precision.HIGHEST)


def bubble(lesser_disp, greater_disp):
    real_part = lesser_disp[0] * greater_disp[1] + lesser_disp[1] * greater_disp[0]
    imag_part = lesser_disp[1] * greater_disp[1] - lesser_disp[0] * greater_disp[0]
    return jnp.stack([real_part, imag_part])


def local(lesser, greater, site_of):
    forward, mirrored, backward = phase_tables(site_of)
    turned = swap_times(lax.all_to_all(greater, "tm", split_axis=5, concat_axis=4, tiled=True))
    lesser_rows, greater_rows = (
        lax.all_to_all(lesser, "mom", split_axis=4, concat_axis=1, tiled=True),
        lax.all_to_all(turned, "mom", split_axis=4, concat_axis=1, tiled=True),
    )
    product = bubble(transform(forward, lesser_rows), transform(mirrored, greater_rows))
    moved_back = transform(backward, product)
    return lax.all_to_all(moved_back, "mom", split_axis=1, concat_axis=4, tiled=True)


def solution(mesh):
    in_specs = (P(None, "mom", None, None, "tm", None), P(None, "mom", None, None, "tm", None), P())
    out_specs = P(None, "mom", None, None, "tm", None)
    return jax.shard_map(local, mesh=mesh, in_specs=in_specs, out_specs=out_specs, check_vma=False)
```

profile of v0, /device:TPU:24, one launch (start us, length us, event | category | flops | bytes accessed | tf_op | source)
XLA Modules:
  0.0 362.2 jit_solution(4848636579083608417)
XLA Ops:
  0.0 14.5 %copy.23 = f32[2,16,2,2,32,256]{4,1,3,2,0,5:T(8,128)} copy(f32[2,16,2,2,32,256]{5,4,3,2,1,0:T(8,128)} %param.4) | data formatting | bytes 8388608 | tf_op args[1]
  14.5 12.8 %reshape.134 = f32[8,1,131072]{2,1,0:T(1,128)} reshape(f32[256,2,2,2,16,32]{5,4,3,2,1,0:T(8,128)} %bitcast.43) | data formatting | bytes 8388608
  27.3 8.0 %all-to-all-start.1 = ((f32[8,1,131072]{2,1,0:T(1,128)}), f32[8,1,131072]{2,1,0:T(1,128)}, u32[]{:S(2)}, u32[]{:S(2)}) async-start(f32[8,1,131072]{2,1,0:T(1,128)} %reshape.134), calls=%async_computation.1 | async-start | bytes 8388608 | tf_op jit(solution)/shard_map/all_to_all | solution.py:55
  35.3 6.6 %copy.21 = f32[2,16,2,2,32,256]{5,1,3,2,0,4:T(8,128)} copy(f32[2,16,2,2,32,256]{5,4,3,2,1,0:T(8,128)} %param.3) | data formatting | bytes 8388608 | tf_op args[0]
  41.9 54.6 %all-to-all-done.1 = f32[8,1,131072]{2,1,0:T(1,128)} async-done(((f32[8,1,131072]{2,1,0:T(1,128)}), f32[8,1,131072]{2,1,0:T(1,128)}, u32[]{:S(2)}, u32[]{:S(2)}) %all-to-all-start.1) | async-done | bytes 4194336 | tf_op jit(solution)/shard_map/all_to_all | solution.py:55
  96.5 5.1 %all-to-all-start = ((f32[2,16,2,2,32,256]{5,1,3,2,0,4:T(8,128)}), f32[2,16,2,2,32,256]{5,1,3,2,0,4:T(8,128)}, u32[]{:S(2)}, u32[]{:S(2)}) async-start(f32[2,16,2,2,32,256]{5,1,3,2,0,4:T(8,128)} %copy.21), calls=%async_computation | async-start | bytes 8388608 | tf_op jit(solution)/shard_map/all_to_all | solution.py:57
  102.1 13.7 %reduce = f32[8,131072]{1,0:T(8,128)} reduce(f32[8,1,131072]{2,1,0:T(1,128)} %all-to-all-done.1, f32[]{:T(128)} %broadcast.105), dimensions={1}, to_apply=%all_to_all.51.reduce_sub_computation | reduce | bytes 8388612 | tf_op jit(solution)/shard_map/all_to_all | solution.py:55
  115.9 13.4 %reshape.135 = f32[256,2,2,2,16,32]{5,4,3,2,1,0:T(8,128)} reshape(f32[8,131072]{1,0:T(8,128)} %reduce) | data formatting | bytes 8388608
  129.2 17.7 %copy.35 = f32[2,16,2,2,32,8,32]{4,5,6,3,2,1,0:T(8,128)} copy(f32[2,16,2,2,32,8,32]{4,1,3,2,0,6,5:T(8,128)} %bitcast.44) | data formatting | bytes 8388608 | tf_op jit(solution)/shard_map/all_to_all | solution.py:55
  147.0 12.6 %all_to_all.54 = f32[2,16,2,2,256,32]{4,5,3,2,1,0:T(8,128)} reshape(f32[2,16,2,2,8,32,32]{5,4,6,3,2,1,0:T(8,128)} %bitcast.45) | data formatting | bytes 8388608 | tf_op jit(solution)/shard_map/all_to_all | solution.py:55
  159.5 4.4 %convolution_bitcast_fusion = f32[2,16,2,2,32,256]{5,4,2,3,1,0:T(8,128)S(1)} fusion(f32[2,16,2,2,256,32]{4,5,3,2,1,0:T(8,128)} %all_to_all.54), kind=kOutput, calls=%fused_computation.4 | convolution fusion | flops 402654208 | bytes 8388608 | tf_op jit(solution)/shard_map/ckabtu,su->ckbast/dot_general | solution.py:44
  164.0 5.2 %copy.25 = f32[2,16,2,2,32,256]{5,2,3,1,0,4:T(2,128)} copy(f32[2,16,2,2,32,256]{5,4,2,3,1,0:T(8,128)S(1)} %convolution_bitcast_fusion) | data formatting | bytes 8388608 | tf_op jit(solution)/shard_map/ckabtu,su->ckbast/transpose | solution.py:44
  169.2 6.0 %all-to-all-start.2 = ((f32[2,16,2,2,32,256]{5,2,3,1,0,4:T(2,128)}), f32[2,16,2,2,32,256]{5,2,3,1,0,4:T(2,128)}, u32[]{:S(2)}, u32[]{:S(2)}) async-start(f32[2,16,2,2,32,256]{5,2,3,1,0,4:T(2,128)} %copy.25), calls=%async_computation.2 | async-start | bytes 8388608 | tf_op jit(solution)/shard_map/all_to_all | solution.py:58
  175.3 2.2 sine_multiply_fusion
  177.6 7.5 %copy.37 = f32[2,16,2,2,16,2,256]{6,5,3,2,1,4,0:T(2,128)} copy(f32[2,16,2,2,16,2,256]{6,1,3,2,0,5,4:T(8,128)} %bitcast.3) | data formatting | bytes 8388608 | tf_op jit(solution)/shard_map/all_to_all | solution.py:57
  185.1 6.4 %reshape.128 = f32[512,2048]{1,0:T(8,128)} reshape(f32[2,16,16,2,2,2,256]{6,5,4,3,2,1,0:T(2,128)} %bitcast.47) | data formatting | bytes 8388608 | tf_op jit(solution)/shard_map/reshape | solution.py:37
  191.5 10.3 %fusion.1 = f32[512,2048]{1,0:T(8,128)} fusion(f32[512,2048]{1,0:T(8,128)} %reshape.128, f32[256,256]{1,0:T(8,128)S(1)} %get-tuple-element.11, f32[256,256]{1,0:T(8,128)S(1)} %get-tuple-element.7, f32[256,256]{1,0:T(8,128)S(1)} %get-tuple-element.8), kind=kOutput, calls=%fused_computation.12 | convolution fusion | flops 6443237376 | bytes 9175040 | tf_op jit(solution)/shard_map/dot_general | solution.py:38
  201.9 25.8 %all-to-all-done.2 = f32[2,16,2,2,32,256]{5,2,3,1,0,4:T(2,128)} async-done(((f32[2,16,2,2,32,256]{5,2,3,1,0,4:T(2,128)}), f32[2,16,2,2,32,256]{5,2,3,1,0,4:T(2,128)}, u32[]{:S(2)}, u32[]{:S(2)}) %all-to-all-start.2) | async-done | bytes 4194336 | tf_op jit(solution)/shard_map/all_to_all | solution.py:58
  227.6 7.7 %copy.36 = f32[2,16,2,2,16,2,256]{6,5,3,2,1,4,0:T(2,128)} copy(f32[2,16,2,2,16,2,256]{6,2,3,1,0,5,4:T(2,128)} %bitcast.10) | data formatting | bytes 8388608 | tf_op jit(solution)/shard_map/all_to_all | solution.py:58
  235.3 6.4 %reshape.129 = f32[512,2048]{1,0:T(8,128)} reshape(f32[2,16,16,2,2,2,256]{6,5,4,3,2,1,0:T(2,128)} %bitcast.48) | data formatting | bytes 8388608 | tf_op jit(solution)/shard_map/reshape | solution.py:37
  241.8 8.9 %fusion.4 = f32[512,2048]{1,0:T(8,128)S(1)} fusion(f32[512,2048]{1,0:T(8,128)} %reshape.129, f32[256,256]{1,0:T(8,128)S(1)} %get-tuple-element.11, f32[256,256]{1,0:T(8,128)S(1)} %get-tuple-element.8, f32[256,256]{1,0:T(8,128)S(1)} %get-tuple-element.7), kind=kOutput, calls=%fused_computation.14 | convolution fusion | flops 6443237376 | bytes 9175040 | tf_op jit(solution)/shard_map/dot_general | solution.py:38
  250.7 2.2 multiply_add_fusion
  252.9 4.0 %add.59 = f32[1,256,2,2,2,256]{5,4,3,2,1,0:T(2,128)} reshape(f32[256,2048]{1,0:T(8,128)} %get-tuple-element.5) | data formatting | bytes 4194304 | tf_op jit(solution)/shard_map/add | solution.py:48
  256.9 3.0 sub.28
  259.9 6.2 %pad_maximum_fusion = f32[2,256,2,2,2,256]{5,4,3,2,1,0:T(2,128)} fusion(f32[1,256,2,2,2,256]{5,4,3,2,1,0:T(2,128)} %sub.28, f32[1,256,2,2,2,256]{5,4,3,2,1,0:T(2,128)} %add.59), kind=kLoop, calls=%fused_computation.1 | loop fusion | flops 1048576 | bytes 8388608 | tf_op jit(solution)/shard_map/stack | solution.py:50
  266.1 6.4 %reshape.130 = f32[512,2048]{1,0:T(8,128)} reshape(f32[2,256,2,2,2,256]{5,4,3,2,1,0:T(2,128)} %pad_maximum_fusion) | data formatting | bytes 8388608 | tf_op jit(solution)/shard_map/reshape | solution.py:37
  272.5 5.3 %copy.27 = f32[512,2048]{0,1:T(8,128)} copy(f32[512,2048]{1,0:T(8,128)} %reshape.130) | data formatting | bytes 8388608 | tf_op jit(solution)/shard_map/reshape | solution.py:37
  277.8 8.8 %fusion.24 = f32[2,256,2,2,2,256]{5,1,4,3,2,0:T(8,128)S(1)} fusion(f32[2,256,512,1,1,1]{2,1,5,4,3,0:T(8,128)S(1)} %bitcast.50, f32[2,2,2,256,512,1]{4,3,2,1,0,5:T(8,128)} %bitcast.46), kind=kOutput, calls=%fused_computation.56 | convolution fusion | flops 6442450944 | bytes 9437184 | tf_op jit(solution)/shard_map/dot_general | solution.py:38
  286.6 3.2 copy.28
  289.9 61.7 %all_to_all.66 = f32[2,256,2,2,2,256]{5,4,3,2,0,1:T(2,128)S(1)} all-to-all(f32[2,256,2,2,2,256]{5,4,3,2,0,1:T(2,128)S(1)} %copy.28), channel_id=1, replica_groups=mesh['mom'=16,'tm'=8] {'mom'}, dimensions={1} | all-to-all | bytes 8388608 | tf_op jit(solution)/shard_map/all_to_all | solution.py:62
  351.6 4.4 %copy.29 = f32[2,16,2,2,16,2,256]{6,5,4,3,2,1,0:T(2,128)} copy(f32[2,16,2,2,16,2,256]{6,5,3,2,0,1,4:T(2,128)S(1)} %bitcast.49) | data formatting | bytes 8388608 | tf_op jit(solution)/shard_map/all_to_all | solution.py:62
  355.9 6.0 %all_to_all.61 = f32[2,16,2,2,32,256]{5,4,3,2,1,0:T(8,128)} reshape(f32[2,16,2,2,16,2,256]{6,5,4,3,2,1,0:T(2,128)} %copy.29) | data formatting | bytes 8388608 | tf_op jit(solution)/shard_map/all_to_all | solution.py:62
  (9 shorter events, 0.7 us)
Async XLA Ops:
  27.3 69.2 %all-to-all-start.1 = ((f32[8,1,131072]{2,1,0:T(1,128)}), f32[8,1,131072]{2,1,0:T(1,128)}, u32[]{:S(2)}, u32[]{:S(2)}) async-start(f32[8,1,131072]{2,1,0:T(1,128)} %reshape.134), calls=%async_computation.1 | async-start | bytes 8388608 | tf_op jit(solution)/shard_map/all_to_all | solution.py:55
  96.5 72.7 %all-to-all-start = ((f32[2,16,2,2,32,256]{5,1,3,2,0,4:T(8,128)}), f32[2,16,2,2,32,256]{5,1,3,2,0,4:T(8,128)}, u32[]{:S(2)}, u32[]{:S(2)}) async-start(f32[2,16,2,2,32,256]{5,1,3,2,0,4:T(8,128)} %copy.21), calls=%async_computation | async-start | bytes 8388608 | tf_op jit(solution)/shard_map/all_to_all | solution.py:57
  169.2 6.0 %copy-start.1 = (s32[256]{0:T(256)S(1)}, s32[256]{0:T(256)}, u32[]{:S(2)}) copy-start(s32[256]{0:T(256)} %param.5) | copy-start | bytes 3076
  169.2 58.4 %all-to-all-start.2 = ((f32[2,16,2,2,32,256]{5,2,3,1,0,4:T(2,128)}), f32[2,16,2,2,32,256]{5,2,3,1,0,4:T(2,128)}, u32[]{:S(2)}, u32[]{:S(2)}) async-start(f32[2,16,2,2,32,256]{5,2,3,1,0,4:T(2,128)} %copy.25), calls=%async_computation.2 | async-start | bytes 8388608 | tf_op jit(solution)/shard_map/all_to_all | solution.py:58
  241.8 8.9 %copy-start = (f32[512,2048]{1,0:T(8,128)S(1)}, f32[512,2048]{1,0:T(8,128)}, u32[]{:S(2)}) copy-start(f32[512,2048]{1,0:T(8,128)} %fusion.1) | copy-start | bytes 12582916
where the time goes:
time: 368 us; the launch traced here: 362 us
  local copies, waits for them, and re-layouts  144 us (39%)
  waiting for transfers between devices  80.4 us (22%)
  blocking collectives  61.7 us (17%)
  matrix products  32.5 us (9%)
  other arithmetic  24.4 us (7%)
  starting transfers between devices  19.1 us (5%)
    all_to_all x1, blocking collectives, local(): lax.all_to_all(moved_back, 'mom', split_axis=1, concat_axis=4, tiled=True)  61.7 us
    all_to_all x1, waiting for transfers between devices, local(): lax.all_to_all(greater, 'tm', split_axis=5, concat_axis=4, tiled=True)  54.6 us
    unnamed x8, local copies, waits for them, and re-layouts  47.3 us
    all_to_all x3, local copies, waits for them, and re-layouts, local(): lax.all_to_all(greater, 'tm', split_axis=5, concat_axis=4, tiled=True)  30.8 us
    dot_general x3, matrix products, transform(): jnp.dot(matrix, flattened, precision=lax.Precision.HIGHEST).reshape(dims_in)  28.1 us
    all_to_all x1, waiting for transfers between devices, local(): lax.all_to_all(turned, 'mom', split_axis=4, concat_axis=1, tiled=True)  25.8 us
    reshape x4, local copies, waits for them, and re-layouts, transform(): flattened = values.reshape(dims_in[0] * dims_in[1], -1)  24.6 us
    all_to_all x1, other arithmetic, local(): lax.all_to_all(greater, 'tm', split_axis=5, concat_axis=4, tiled=True)  13.7 us
  transfers between devices with their start and end apart: 3, of which 2 were waited for; matrix products, arithmetic and copies ran while one was open for 24% of the time, Pallas kernels for 0%

commit v1 on v0

v1 whole, which is shorter than its diff:
```python
import math

import jax
import jax.numpy as jnp
from jax import lax
from jax.experimental import pallas as pl
from jax.experimental.pallas import tpu as pltpu
from jax.sharding import PartitionSpec as P

L = 16
VMEM = 48 * 1024 * 1024
F32 = jnp.float32
BF16 = jnp.bfloat16


def params():
    return pltpu.CompilerParams(vmem_limit_bytes=VMEM)


def phase_tables(site_of):
    momenta = site_of.shape[0]
    lattice = jnp.arange(momenta, dtype=jnp.int32)
    turn_count = (
        (lattice // L)[:, None] * (site_of // L)[None, :]
        + (lattice % L)[:, None] * (site_of % L)[None, :]
    ) % L
    angles = turn_count.astype(F32) * (2.0 * math.pi / L)
    scaling = 1.0 / math.sqrt(momenta)
    cosine = (jnp.cos(angles) * scaling).reshape(momenta, 16, 1, 16)
    sine = (jnp.sin(angles) * scaling).reshape(momenta, 16, 1, 16)
    forward = jnp.stack(
        [jnp.concatenate([cosine, -sine], 2), jnp.concatenate([sine, cosine], 2)], 0
    ).reshape(2 * momenta, 2 * momenta)
    mirrored = jnp.stack(
        [jnp.concatenate([cosine, sine], 2), jnp.concatenate([-sine, cosine], 2)], 0
    ).reshape(2 * momenta, 2 * momenta)
    return forward, mirrored, forward.T


def split(x):
    high = x.astype(BF16)
    return high, (x - high.astype(F32)).astype(BF16)


def load_time(ref, t):
    return jnp.concatenate([ref[pl.ds(8 * h + t, 512, stride=16), :] for h in range(2)], 1)


def store_table(table_ref, cat_ref):
    n = table_ref.shape[1]
    high, low = split(table_ref[...])
    cat_ref[:, 0:n] = high
    cat_ref[:, n : 2 * n] = high
    cat_ref[:, 2 * n : 3 * n] = low


def times(cat_ref, x):
    high, low = split(x)
    return jnp.dot(
        cat_ref[...], jnp.concatenate([high, low, high], 0), preferred_element_type=F32
    )


def pack_lesser_body(i_ref, o_ref):
    for g in range(4):
        for h in range(2):
            o_ref[g, 0, :, h] = i_ref[0, :, 0, 8 * g : 8 * g + 8, 128 * h : 128 * h + 128]


def pack_lesser(values):
    return pl.pallas_call(
        pack_lesser_body,
        grid=(2, 4),
        in_specs=[pl.BlockSpec((1, 16, 1, 32, 256), lambda c, o: (c, 0, o, 0, 0))],
        out_specs=pl.BlockSpec((4, 1, 16, 2, 8, 128), lambda c, o: (o, c, 0, 0, 0, 0)),
        out_shape=jax.ShapeDtypeStruct((16, 2, 16, 2, 8, 128), F32),
        compiler_params=params(),
    )(values)


def pack_greater_body(i_ref, o_ref):
    for q in range(4):
        for h in range(2):
            block = i_ref[0, 4 * q : 4 * q + 4, 0, :, 128 * h : 128 * h + 128]
            turned = block.reshape(128, 128).T
            for s in range(4):
                for g in range(4):
                    r = 32 * s + 8 * g
                    o_ref[0, g, 4 * h + s, 0, q] = turned[r : r + 8, :]


def pack_greater(values):
    return pl.pallas_call(
        pack_greater_body,
        grid=(2, 4),
        in_specs=[
            pl.BlockSpec((1, 16, 1, 32, 256), lambda c, o: (c, 0, (o % 2) * 2 + o // 2, 0, 0))
        ],
        out_specs=pl.BlockSpec((1, 4, 8, 1, 4, 8, 128), lambda c, o: (o, 0, 0, c, 0, 0, 0)),
        out_shape=jax.ShapeDtypeStruct((4, 4, 8, 2, 4, 8, 128), F32),
        compiler_params=params(),
    )(values)


def lesser_body(x_ref, table_ref, o_ref, cat_ref):
    t = pl.program_id(0)

    @pl.when(t == 0)
    def _():
        store_table(table_ref, cat_ref)

    o_ref[0] = times(cat_ref, load_time(x_ref, t))


def lesser_transform(rows, table):
    return pl.pallas_call(
        lesser_body,
        grid=(8,),
        in_specs=[
            pl.BlockSpec((8192, 128), lambda t: (0, 0)),
            pl.BlockSpec((512, 512), lambda t: (0, 0)),
        ],
        out_specs=pl.BlockSpec((1, 512, 256), lambda t: (t, 0, 0)),
        out_shape=jax.ShapeDtypeStruct((8, 512, 256), F32),
        scratch_shapes=[pltpu.VMEM((512, 1536), BF16)],
        compiler_params=params(),
        cost_estimate=pl.CostEstimate(
            flops=2 * 512 * 1536 * 2048, bytes_accessed=9 << 20, transcendentals=0
        ),
    )(rows, table)


def swap_blocks(tiles):
    lane = lax.broadcasted_iota(jnp.int32, tiles[0].shape, 1)
    a, b, c, d = tiles
    low = lane < 64
    pairs = []
    for p, q in ((a, c), (b, d)):
        pairs.append(jnp.where(low, p, pltpu.roll(q, 64, 1)))
        pairs.append(jnp.where(low, pltpu.roll(p, 64, 1), q))
    e, f, g, h = pairs[0], pairs[2], pairs[1], pairs[3]
    even = (lane // 32) % 2 == 0
    return (
        jnp.where(even, e, pltpu.roll(f, 32, 1)),
        jnp.where(even, pltpu.roll(e, 96, 1), f),
        jnp.where(even, g, pltpu.roll(h, 32, 1)),
        jnp.where(even, pltpu.roll(g, 96, 1), h),
    )


def bubble_body(x_ref, l_ref, mirrored_ref, backward_ref, o_ref, g_ref, mcat_ref, bcat_ref):
    t = pl.program_id(0)

    @pl.when(t == 0)
    def _():
        store_table(mirrored_ref, mcat_ref)
        store_table(backward_ref, bcat_ref)

        def shard(m, carry):
            for c in range(2):
                for h in range(2):
                    tiles = [x_ref[m, 4 * h + s, c].reshape(32, 128) for s in range(4)]
                    for k, tile in enumerate(swap_blocks(tiles)):
                        for q in range(4):
                            row = ((m * 2 + c) * 16 + 4 * q + k) * 16 + 8 * h
                            g_ref[pl.ds(pl.multiple_of(row, 8), 8), :] = tile[8 * q : 8 * q + 8]
            return carry

        lax.fori_loop(0, 16, shard, 0)

    greater = times(mcat_ref, load_time(g_ref, t))
    lr, li = l_ref[0, 0:256], l_ref[0, 256:512]
    gr, gi = greater[0:256], greater[256:512]
    product = jnp.concatenate([lr * gi + li * gr, li * gi - lr * gr], 0)
    result = times(bcat_ref, product)
    for h in range(2):
        o_ref[pl.ds(8 * h + t, 512, stride=16), :] = result[:, 128 * h : 128 * h + 128]


def bubble(greater, lesser_disp, mirrored, backward):
    return pl.pallas_call(
        bubble_body,
        grid=(8,),
        in_specs=[
            pl.BlockSpec((16, 8, 2, 4, 8, 128), lambda t: (0,) * 6),
            pl.BlockSpec((1, 512, 256), lambda t: (t, 0, 0)),
            pl.BlockSpec((512, 512), lambda t: (0, 0)),
            pl.BlockSpec((512, 512), lambda t: (0, 0)),
        ],
        out_specs=pl.BlockSpec((8192, 128), lambda t: (0, 0)),
        out_shape=jax.ShapeDtypeStruct((8192, 128), F32),
        scratch_shapes=[
            pltpu.VMEM((8192, 128), F32),
            pltpu.VMEM((512, 1536), BF16),
            pltpu.VMEM((512, 1536), BF16),
        ],
        compiler_params=params(),
        cost_estimate=pl.CostEstimate(
            flops=4 * 512 * 1536 * 2048, bytes_accessed=14 << 20, transcendentals=0
        ),
    )(greater, lesser_disp, mirrored, backward)


def unpack_body(i_ref, o_ref):
    for g in range(4):
        for h in range(2):
            o_ref[0, :, 0, 8 * g : 8 * g + 8, 128 * h : 128 * h + 128] = i_ref[g, 0, :, h]


def unpack(values):
    return pl.pallas_call(
        unpack_body,
        grid=(2, 4),
        in_specs=[pl.BlockSpec((4, 1, 16, 2, 8, 128), lambda c, o: (o, c, 0, 0, 0, 0))],
        out_specs=pl.BlockSpec((1, 16, 1, 32, 256), lambda c, o: (c, 0, o, 0, 0)),
        out_shape=jax.ShapeDtypeStruct((2, 16, 4, 32, 256), F32),
        compiler_params=params(),
    )(values)


def local(lesser, greater, site_of):
    shape = lesser.shape
    merged = (2, 16, 4, 32, 256)
    lesser_out = pack_lesser(lesser.reshape(merged)).reshape(16, 512, 128)
    lesser_rows = lax.all_to_all(lesser_out, "mom", 0, 0, tiled=True).reshape(8192, 128)
    greater_out = pack_greater(greater.reshape(merged)).reshape(128, 64, 128)
    greater_rows = lax.all_to_all(greater_out, ("mom", "tm"), 0, 0, tiled=True)
    forward, mirrored, backward = phase_tables(site_of)
    lesser_disp = lesser_transform(lesser_rows, forward)
    moved = bubble(greater_rows.reshape(16, 8, 2, 4, 8, 128), lesser_disp, mirrored, backward)
    back = lax.all_to_all(moved.reshape(16, 512, 128), "mom", 0, 0, tiled=True)
    return unpack(back.reshape(16, 2, 16, 2, 8, 128)).reshape(shape)


def solution(mesh):
    in_specs = (P(None, "mom", None, None, "tm", None), P(None, "mom", None, None, "tm", None), P())
    out_specs = P(None, "mom", None, None, "tm", None)
    return jax.shard_map(local, mesh=mesh, in_specs=in_specs, out_specs=out_specs, check_vma=False)
```

time: 368 us -> 219 us (0.60); the launches traced: 362 us -> 219 us
  local copies, waits for them, and re-layouts: 144 us -> 8.63 us
  Pallas kernels: 0 us -> 47.8 us
  matrix products: 32.5 us -> 0 us
  other arithmetic: 24.4 us -> 2.38 us
  blocking collectives: 61.7 us -> 56.2 us
    all_to_all x7 -> x0, local copies, waits for them, and re-layouts: 56.5 us -> none  [the longest x3 30.8 us: local(): lax.all_to_all(greater, 'tm', split_axis=5, concat_axis=4, tiled=True)]
    pallas_call x0 -> x5, Pallas kernels: none -> 47.8 us  [the longest x1 25.6 us: bubble(): pl.pallas_call(bubble_body, grid=(8,), in_specs=[pl.BlockSpec((16, 8, 2,...]
    unnamed x8 -> x10, local copies, waits for them, and re-layouts: 47.3 us -> 6.06 us
    dot_general x4 -> x0, matrix products: 32.5 us -> none  [the longest x3 28.1 us: transform(): jnp.dot(matrix, flattened, precision=lax.Precision.HIGHEST).reshape(dims_in)]
    reshape x4 -> x2, local copies, waits for them, and re-layouts: 24.6 us -> 0.66 us  [the longest x1 0.33 us: phase_tables(): mirrored = jnp.stack([jnp.concatenate([cosine, sine], 2), jnp.concatenate...]
    all_to_all x1 -> x0, other arithmetic: 13.7 us -> none  [local(): lax.all_to_all(greater, 'tm', split_axis=5, concat_axis=4, tiled=True)]
    all_to_all x1, blocking collectives: 61.7 us -> 56.2 us  [local(): back = lax.all_to_all(moved.reshape(16, 512, 128), 'mom', 0, 0, tiled=True)]
    transpose x1 -> x0, local copies, waits for them, and re-layouts: 5.25 us -> none  [swap_times(): jnp.einsum('ckabtu,su->ckbast', values, identity, precision=lax.Precision...]
  transfers between devices with their start and end apart: 3 -> 2, of which waited for: 2 -> 2; matrix products, arithmetic and copies ran while one was open for 24% -> 2% of each run, Pallas kernels for 0% -> 6%
where the time goes in v1:
time: 219 us
  waiting for transfers between devices  81.2 us (37%)
  blocking collectives  56.2 us (26%)
  Pallas kernels  47.8 us (22%)
  starting transfers between devices  22.5 us (10%)
  local copies, waits for them, and re-layouts  8.63 us (4%)
  other arithmetic  2.38 us (1%)
    all_to_all x1, blocking collectives, local(): back = lax.all_to_all(moved.reshape(16, 512, 128), 'mom', 0, 0, tiled=True)  56.2 us
    all_to_all x1, waiting for transfers between devices, local(): lax.all_to_all(lesser_out, 'mom', 0, 0, tiled=True).reshape(8192, 128)  44.7 us
    all_to_all x1, waiting for transfers between devices, local(): greater_rows = lax.all_to_all(greater_out, ('mom', 'tm'), 0, 0, tiled=True)  36.4 us
    pallas_call x1, Pallas kernels, bubble(): pl.pallas_call(bubble_body, grid=(8,), in_specs=[pl.BlockSpec((16, 8, 2,...  25.6 us
    all_to_all x1, starting transfers between devices, local(): greater_rows = lax.all_to_all(greater_out, ('mom', 'tm'), 0, 0, tiled=True)  16.7 us
    pallas_call x1, Pallas kernels, lesser_transform(): pl.pallas_call(lesser_body, grid=(8,), in_specs=[pl.BlockSpec((8192, 128)...  8 us
    unnamed x10, local copies, waits for them, and re-layouts  6.06 us
    all_to_all x1, starting transfers between devices, local(): lax.all_to_all(lesser_out, 'mom', 0, 0, tiled=True).reshape(8192, 128)  5.81 us
  transfers between devices with their start and end apart: 2, of which 2 were waited for; matrix products, arithmetic and copies ran while one was open for 2% of the time, Pallas kernels for 6%

profile of v1, /device:TPU:24, one launch (start us, length us, event | category | flops | bytes accessed | tf_op | source)
XLA Modules:
  0.0 218.8 jit_solution(6171247060978206247)
XLA Ops:
  0.0 4.8 %shard_map.38 = f32[16,2,16,2,8,128]{5,4,3,2,1,0:T(8,128)S(1)} custom-call(f32[2,16,4,32,256]{4,3,2,1,0:T(8,128)} %bitcast.36), custom_call_target="tpu_custom_call" | custom-call | tf_op jit(solution)/shard_map/pallas_call | solution.py:71
  4.8 0.0 copy-start.1
  4.8 1.9 copy-done.1
  6.8 5.8 %all-to-all-start.1 = ((f32[16,512,128]{2,1,0:T(8,128)}), f32[16,512,128]{2,1,0:T(8,128)}, u32[]{:S(2)}, u32[]{:S(2)}) async-start(f32[16,512,128]{2,1,0:T(8,128)} %bitcast.32), calls=%async_computation.1 | async-start | bytes 8388608 | tf_op jit(solution)/shard_map/all_to_all | solution.py:225
  12.6 5.7 %shard_map.37 = f32[4,4,8,2,4,8,128]{6,5,4,3,2,1,0:T(8,128)S(1)} custom-call(f32[2,16,4,32,256]{4,3,2,1,0:T(8,128)} %bitcast.37), custom_call_target="tpu_custom_call" | custom-call | tf_op jit(solution)/shard_map/pallas_call | solution.py:93
  18.3 0.0 copy-start
  18.3 2.0 copy-done
  20.3 44.7 %all-to-all-done.1 = f32[16,512,128]{2,1,0:T(8,128)} async-done(((f32[16,512,128]{2,1,0:T(8,128)}), f32[16,512,128]{2,1,0:T(8,128)}, u32[]{:S(2)}, u32[]{:S(2)}) %all-to-all-start.1) | async-done | bytes 4194336 | tf_op jit(solution)/shard_map/all_to_all | solution.py:225
  65.0 0.0 copy-start.3
  65.0 16.7 %all-to-all-start = ((f32[128,64,128]{2,1,0:T(8,128)}), f32[128,64,128]{2,1,0:T(8,128)}, u32[]{:S(2)}, u32[]{:S(2)}) async-start(f32[128,64,128]{2,1,0:T(8,128)} %bitcast.31), calls=%async_computation | async-start | bytes 8388608 | tf_op jit(solution)/shard_map/all_to_all | solution.py:227
  81.7 0.0 copy-done.3
  81.7 0.1 mul.110
  81.8 0.1 mul.114
  81.9 1.2 fusion.6
  83.0 0.1 fusion.2
  83.2 0.5 copy.9
  83.7 0.4 stack.22
  84.1 1.0 pad_maximum_fusion.1
  85.1 0.1 copy.12
  85.2 0.3 copy.10.mirrored_ref
  85.5 0.1 pad_maximum_fusion
  85.6 0.8 copy.7
  86.5 0.1 copy.11
  86.5 0.3 copy.8.table_ref
  86.9 8.0 %shard_map.39.l_ref = f32[8,512,256]{2,1,0:T(8,128)S(1)} custom-call(f32[8192,128]{1,0:T(8,128)} %bitcast.5.x_ref, f32[512,512]{1,0:T(8,128)S(1)} %copy.8.table_ref), custom_call_target="tpu_custom_call" | custom-call | flops 3221225472 | bytes 9437184 | tf_op jit(solution)/shard_map/pallas_call | solution.py:116
  94.9 0.0 copy-start.2
  94.9 2.0 copy-done.2
  96.9 36.4 %all-to-all-done = f32[128,64,128]{2,1,0:T(8,128)} async-done(((f32[128,64,128]{2,1,0:T(8,128)}), f32[128,64,128]{2,1,0:T(8,128)}, u32[]{:S(2)}, u32[]{:S(2)}) %all-to-all-start) | async-done | bytes 4194336 | tf_op jit(solution)/shard_map/all_to_all | solution.py:227
  133.3 25.6 %shard_map.40 = f32[8192,128]{1,0:T(8,128)} custom-call(f32[16,8,2,4,8,128]{5,4,3,2,1,0:T(8,128)} %bitcast.2.x_ref, f32[8,512,256]{2,1,0:T(8,128)} %copy-done.2, f32[512,512]{1,0:T(8,128)S(1)} %copy.10.mirrored_ref, f32[512,512]{1,0:T(8,128)S(1)} %bitcast.35), custom_call_target="tpu_custom_call" | custom-call | flops 6442450944 | bytes 14680064 | tf_op jit(solution)/shard_map/pallas_call | solution.py:181
  158.9 56.2 %all_to_all.15 = f32[16,512,128]{2,1,0:T(8,128)S(1)} all-to-all(f32[16,512,128]{2,1,0:T(8,128)} %bitcast.38), channel_id=1, replica_groups=mesh['mom'=16,'tm'=8] {'mom'}, dimensions={0} | all-to-all | bytes 8388608 | tf_op jit(solution)/shard_map/all_to_all | solution.py:231
  215.1 3.8 %shard_map.41 = f32[2,16,4,32,256]{4,3,2,1,0:T(8,128)} custom-call(f32[16,2,16,2,8,128]{5,4,3,2,1,0:T(8,128)S(1)} %bitcast.33), custom_call_target="tpu_custom_call" | custom-call | tf_op jit(solution)/shard_map/pallas_call | solution.py:211
  (2 shorter events, 0.0 us)
Async XLA Ops:
  4.8 2.0 copy-start.1
  6.8 58.2 %all-to-all-start.1 = ((f32[16,512,128]{2,1,0:T(8,128)}), f32[16,512,128]{2,1,0:T(8,128)}, u32[]{:S(2)}, u32[]{:S(2)}) async-start(f32[16,512,128]{2,1,0:T(8,128)} %bitcast.32), calls=%async_computation.1 | async-start | bytes 8388608 | tf_op jit(solution)/shard_map/all_to_all | solution.py:225
  18.3 2.0 copy-start
  65.0 16.7 %copy-start.3 = (s32[256]{0:T(256)S(1)}, s32[256]{0:T(256)}, u32[]{:S(2)}) copy-start(s32[256]{0:T(256)} %param.5) | copy-start | bytes 3076
  65.0 68.3 %all-to-all-start = ((f32[128,64,128]{2,1,0:T(8,128)}), f32[128,64,128]{2,1,0:T(8,128)}, u32[]{:S(2)}, u32[]{:S(2)}) async-start(f32[128,64,128]{2,1,0:T(8,128)} %bitcast.31), calls=%async_computation | async-start | bytes 8388608 | tf_op jit(solution)/shard_map/all_to_all | solution.py:227
  94.9 2.0 copy-start.2

commit v2 on v0

v2 whole, which is shorter than its diff:
```python
import math

import jax
import jax.numpy as jnp
from jax import lax
from jax.experimental import pallas as pl
from jax.experimental.pallas import tpu as pltpu
from jax.sharding import PartitionSpec as P

L = 16
VMEM = 56 * 1024 * 1024
F32 = jnp.float32
BF16 = jnp.bfloat16
BLOCK = (2, 16, 8, 128)
ANY = pl.BlockSpec(memory_space=pl.ANY)
HBM = pl.BlockSpec(memory_space=pltpu.HBM)


def params():
    return pltpu.CompilerParams(vmem_limit_bytes=VMEM)


def cost():
    return pl.CostEstimate(flops=1, bytes_accessed=1, transcendentals=0)


def shape(*dims):
    return jax.ShapeDtypeStruct(dims, F32)


def split(x):
    high = x.astype(BF16)
    return high, (x - high.astype(F32)).astype(BF16)


def cosines(turns):
    turns = turns % L
    turns = jnp.where(turns > 8, L - turns, turns)
    near = jnp.where(turns > 4, 8 - turns, turns)
    value = jnp.zeros(turns.shape, F32)
    for step in range(4):
        value = jnp.where(near == step, math.cos(2.0 * math.pi * step / L) / L, value)
    return jnp.where(turns > 4, -value, value)


def phase_turns(lattice, site):
    return (lattice // L) * (site // L) + (lattice % L) * (site % L)


def table_body(lesser_ref, greater_ref, result_ref, *outs):
    rows = lax.broadcasted_iota(jnp.int32, (512, 512), 0)
    columns = lax.broadcasted_iota(jnp.int32, (512, 512), 1)
    forward = phase_turns(rows % 256, lesser_ref[...]) + 4 * ((columns // 16) % 2 - rows // 256)
    mirrored = phase_turns(rows % 256, greater_ref[...]) - 4 * ((columns // 4) % 2 - rows // 256)
    backward = phase_turns(columns % 256, result_ref[...]) + 4 * ((rows // 16) % 2 - columns // 256)
    for out, turns in zip(outs, (forward, mirrored, backward)):
        high, low = split(cosines(turns + L))
        out[:, 0:512] = high
        out[:, 512:1024] = low


def phase_tables(site_of):
    parts = jnp.broadcast_to(site_of.reshape(16, 1, 16), (16, 2, 16))
    columns = parts.reshape(512)
    quads = parts.reshape(16, 2, 4, 4).transpose(3, 0, 1, 2).reshape(1, 512)
    return pl.pallas_call(
        table_body,
        out_shape=(jax.ShapeDtypeStruct((512, 1024), BF16),) * 3,
        compiler_params=params(),
        cost_estimate=cost(),
    )(columns.reshape(1, 512), quads, columns.reshape(512, 1))


def times(table_ref, x):
    high, low = split(x)
    table_high, table_low = table_ref[:, 0:512], table_ref[:, 512:1024]
    product = jnp.dot(table_high, high, preferred_element_type=F32)
    product += jnp.dot(table_high, low, preferred_element_type=F32)
    return product + jnp.dot(table_low, high, preferred_element_type=F32)


def part(ref, m):
    return ref.at[:, :, m // 4, pl.ds(m % 4 * 8, 8), :]


def half(ref, m, h):
    return ref.at[m, :, :, :, pl.ds(128 * h, 128)]


def relay(loads, stores):
    for group in loads:
        for copy in group:
            copy.start()
    for group, after in zip(loads, stores):
        for copy in group:
            copy.wait()
        for copy in after:
            copy.start()
    for group in stores:
        for copy in group:
            copy.wait()


RELAY = [
    pltpu.VMEM((16, 2, 16, 8, 256), F32),
    pltpu.SemaphoreType.DMA((16,)),
    pltpu.SemaphoreType.DMA((16, 2)),
]


def pack_body(i_ref, o_ref, buffer, one, two):
    copy = pltpu.make_async_copy
    relay(
        [[copy(part(i_ref, m), buffer.at[m], one.at[m])] for m in range(16)],
        [
            [copy(half(buffer, m, h), o_ref.at[m, h], two.at[m, h]) for h in range(2)]
            for m in range(16)
        ],
    )


def pack(values):
    return pl.pallas_call(
        pack_body,
        in_specs=[HBM],
        out_specs=HBM,
        out_shape=shape(16, 2, *BLOCK),
        scratch_shapes=RELAY,
        compiler_params=params(),
        cost_estimate=cost(),
    )(values)


def unpack_body(i_ref, o_ref, buffer, one, two):
    copy = pltpu.make_async_copy
    relay(
        [
            [copy(i_ref.at[m, h], half(buffer, m, h), two.at[m, h]) for h in range(2)]
            for m in range(16)
        ],
        [[copy(buffer.at[m], part(o_ref, m), one.at[m])] for m in range(16)],
    )


def unpack(values):
    return pl.pallas_call(
        unpack_body,
        in_specs=[ANY],
        out_specs=HBM,
        out_shape=shape(2, 16, 4, 32, 256),
        scratch_shapes=RELAY,
        compiler_params=params(),
        cost_estimate=cost(),
    )(values)


def swap_rows(tiles):
    tiles = list(tiles)
    row = lax.broadcasted_iota(jnp.int32, tiles[0].shape, 1)
    for step in (4, 2, 1):
        keep = (row // step) % 2 == 0
        for i in range(8):
            if i // step % 2 == 0:
                a, b = tiles[i], tiles[i + step]
                tiles[i] = jnp.where(keep, a, pltpu.roll(b, step, 1))
                tiles[i + step] = jnp.where(keep, pltpu.roll(a, 8 - step, 1), b)
    return tiles


def pack_greater_body(i_ref, o_ref):
    for h in range(2):
        turned = []
        for c in range(2):
            for q in range(4):
                block = i_ref[c, 4 * q : 4 * q + 4, 0, :, 128 * h : 128 * h + 128]
                turned.append(block.reshape(128, 128).T.reshape(16, 8, 128))
        for t, tile in enumerate(swap_rows(turned)):
            for s in range(4):
                for g in range(4):
                    o_ref[0, g, 4 * h + s, t] = tile[4 * s + g]


def pack_greater(values):
    return pl.pallas_call(
        pack_greater_body,
        grid=(4,),
        in_specs=[
            pl.BlockSpec((2, 16, 1, 32, 256), lambda o: (0, 0, (o % 2) * 2 + o // 2, 0, 0))
        ],
        out_specs=pl.BlockSpec((1, 4, 8, 8, 8, 128), lambda o: (o, 0, 0, 0, 0, 0)),
        out_shape=shape(4, 4, 8, 8, 8, 128),
        compiler_params=params(),
        cost_estimate=cost(),
    )(values)


def swap_blocks(tiles):
    lane = lax.broadcasted_iota(jnp.int32, tiles[0].shape, 1)
    a, b, c, d = tiles
    low = lane < 64
    pairs = []
    for p, q in ((a, c), (b, d)):
        pairs.append(jnp.where(low, p, pltpu.roll(q, 64, 1)))
        pairs.append(jnp.where(low, pltpu.roll(p, 64, 1), q))
    e, f, g, h = pairs[0], pairs[2], pairs[1], pairs[3]
    even = (lane // 32) % 2 == 0
    return (
        jnp.where(even, e, pltpu.roll(f, 32, 1)),
        jnp.where(even, pltpu.roll(e, 96, 1), f),
        jnp.where(even, g, pltpu.roll(h, 32, 1)),
        jnp.where(even, pltpu.roll(g, 96, 1), h),
    )


ROWS = pl.BlockSpec((16, 1, 256, 128), lambda h, t: (0, h, 0, 0))
DISP = pl.BlockSpec((1, 1, 512, 256), lambda h, t: (h, t, 0, 0))
TABLE = pl.BlockSpec((512, 1024), lambda h, t: (0, 0))


def lesser_body(x_ref, table_ref, o_ref):
    step = pl.program_id(1)
    rows = x_ref.reshape(4096, 128)
    x = jnp.concatenate([rows[pl.ds(2 * step + i, 512, stride=8), :] for i in range(2)], 1)
    o_ref[0, 0] = times(table_ref, x)


def lesser_transform(rows, table):
    return pl.pallas_call(
        lesser_body,
        grid=(2, 4),
        in_specs=[ROWS, TABLE],
        out_specs=DISP,
        out_shape=shape(2, 4, 512, 256),
        compiler_params=params(),
        cost_estimate=cost(),
    )(rows, table)


def bubble(lesser, greater):
    lr, li = lesser[0:256], lesser[256:512]
    gr, gi = greater[0:256], greater[256:512]
    return jnp.concatenate([lr * gi + li * gr, li * gi - lr * gr], 0)


def bubble_body(x_ref, l_ref, mirrored_ref, backward_ref, o_ref, result_ref):
    step = pl.program_id(1)
    pairs = []
    for i in range(2):
        tiles = [x_ref[:, s, i].reshape(128, 128) for s in range(4)]
        pairs.append(jnp.concatenate(swap_blocks(tiles), 0))
    product = bubble(l_ref[0, 0], times(mirrored_ref, jnp.concatenate(pairs, 1)))
    result = times(backward_ref, product)
    for i in range(2):
        result_ref[2 * step + i] = result[:, 128 * i : 128 * i + 128]

    @pl.when(step == 3)
    def _():
        def shard(m, carry):
            row = pl.multiple_of(32 * m, 32)
            tiles = [result_ref[t, pl.ds(row, 32), :].reshape(4, 8, 128) for t in range(8)]
            o_ref[m, 0] = jnp.stack(swap_rows(tiles), 1).reshape(256, 128)
            return carry

        lax.fori_loop(0, 16, shard, 0)


def bubble_transform(greater, lesser_disp, mirrored, backward):
    return pl.pallas_call(
        bubble_body,
        grid=(2, 4),
        in_specs=[
            pl.BlockSpec((16, 4, 2, 8, 128), lambda h, t: (0, h, t, 0, 0)),
            DISP,
            TABLE,
            TABLE,
        ],
        out_specs=ROWS,
        out_shape=shape(16, 2, 256, 128),
        scratch_shapes=[pltpu.VMEM((8, 512, 128), F32)],
        compiler_params=params(),
        cost_estimate=cost(),
    )(greater, lesser_disp, mirrored, backward)


def local(lesser, greater, site_of):
    merged = (2, 16, 4, 32, 256)
    lesser_out = pack(lesser.reshape(merged)).reshape(16, 512, 128)
    lesser_rows = lax.all_to_all(lesser_out, "mom", 0, 0, tiled=True).reshape(16, 2, 256, 128)
    greater_out = pack_greater(greater.reshape(merged)).reshape(128, 64, 128)
    greater_rows = lax.all_to_all(greater_out, ("mom", "tm"), 0, 0, tiled=True)
    forward, mirrored, backward = phase_tables(site_of)
    disp = lesser_transform(lesser_rows, forward)
    moved = bubble_transform(greater_rows.reshape(16, 8, 8, 8, 128), disp, mirrored, backward)
    back = lax.all_to_all(moved.reshape(16, 512, 128), "mom", 0, 0, tiled=True)
    return unpack(back.reshape(16, 2, *BLOCK)).reshape(lesser.shape)


def solution(mesh):
    in_specs = (P(None, "mom", None, None, "tm", None), P(None, "mom", None, None, "tm", None), P())
    out_specs = P(None, "mom", None, None, "tm", None)
    return jax.shard_map(local, mesh=mesh, in_specs=in_specs, out_specs=out_specs, check_vma=False)
```

time: 368 us -> 214 us (0.58); the launches traced: 362 us -> 213 us
  local copies, waits for them, and re-layouts: 144 us -> 2.75 us
  Pallas kernels: 0 us -> 52.5 us
  matrix products: 32.5 us -> 0 us
  other arithmetic: 24.4 us -> 0 us
  blocking collectives: 61.7 us -> 56.3 us
    all_to_all x7 -> x0, local copies, waits for them, and re-layouts: 56.5 us -> none  [the longest x3 30.8 us: local(): lax.all_to_all(greater, 'tm', split_axis=5, concat_axis=4, tiled=True)]
    pallas_call x0 -> x6, Pallas kernels: none -> 52.5 us  [the longest x1 21.4 us: bubble_transform(): pl.pallas_call(bubble_body, grid=(2, 4), in_specs=[pl.BlockSpec((16, 4, 2...]
    unnamed x8 -> x2, local copies, waits for them, and re-layouts: 47.3 us -> 0.01 us
    dot_general x4 -> x0, matrix products: 32.5 us -> none  [the longest x3 28.1 us: transform(): jnp.dot(matrix, flattened, precision=lax.Precision.HIGHEST).reshape(dims_in)]
    reshape x4 -> x1, local copies, waits for them, and re-layouts: 24.6 us -> 0.73 us  [phase_tables(): quads = parts.reshape(16, 2, 4, 4).transpose(3, 0, 1, 2).reshape(1, 512)]
    all_to_all x1 -> x0, other arithmetic: 13.7 us -> none  [local(): lax.all_to_all(greater, 'tm', split_axis=5, concat_axis=4, tiled=True)]
    another operation x1 -> x0, other arithmetic: 6.18 us -> none  [bubble(): return jnp.stack([real_part, imag_part])]
    all_to_all x1, blocking collectives: 61.7 us -> 56.3 us  [local(): back = lax.all_to_all(moved.reshape(16, 512, 128), 'mom', 0, 0, tiled=True)]
  transfers between devices with their start and end apart: 3 -> 2, of which waited for: 2 -> 2; matrix products, arithmetic and copies ran while one was open for 24% -> 1% of each run, Pallas kernels for 0% -> 11%
where the time goes in v2:
time: 214 us; the launch traced here: 213 us
  waiting for transfers between devices  78.5 us (37%)
  blocking collectives  56.3 us (26%)
  Pallas kernels  52.5 us (25%)
  starting transfers between devices  22.5 us (11%)
  local copies, waits for them, and re-layouts  2.75 us (1%)
    all_to_all x1, blocking collectives, local(): back = lax.all_to_all(moved.reshape(16, 512, 128), 'mom', 0, 0, tiled=True)  56.3 us
    all_to_all x1, waiting for transfers between devices, local(): lax.all_to_all(lesser_out, 'mom', 0, 0, tiled=True).reshape(16, 2, 256, 128)  47 us
    all_to_all x1, waiting for transfers between devices, local(): greater_rows = lax.all_to_all(greater_out, ('mom', 'tm'), 0, 0, tiled=True)  31.6 us
    pallas_call x1, Pallas kernels, bubble_transform(): pl.pallas_call(bubble_body, grid=(2, 4), in_specs=[pl.BlockSpec((16, 4, 2...  21.4 us
    all_to_all x1, starting transfers between devices, local(): greater_rows = lax.all_to_all(greater_out, ('mom', 'tm'), 0, 0, tiled=True)  16.7 us
    pallas_call x1, Pallas kernels, lesser_transform(): pl.pallas_call(lesser_body, grid=(2, 4), in_specs=[ROWS, TABLE], out_spec...  9.52 us
    pallas_call x1, Pallas kernels, phase_tables(): pl.pallas_call(table_body, out_shape=(jax.ShapeDtypeStruct((512, 1024), B...  7.76 us
    all_to_all x1, starting transfers between devices, local(): lax.all_to_all(lesser_out, 'mom', 0, 0, tiled=True).reshape(16, 2, 256, 128)  5.82 us
  transfers between devices with their start and end apart: 2, of which 2 were waited for; matrix products, arithmetic and copies ran while one was open for 1% of the time, Pallas kernels for 11%

profile of v2, /device:TPU:24, one launch (start us, length us, event | category | flops | bytes accessed | tf_op | source)
XLA Modules:
  0.0 212.6 jit_solution(3218693185716274308)
XLA Ops:
  0.0 4.1 %shard_map.38 = f32[16,2,2,16,8,128]{5,4,3,2,1,0:T(8,128)} custom-call(f32[2,16,4,32,256]{4,3,2,1,0:T(8,128)} %bitcast.15), custom_call_target="tpu_custom_call" | custom-call | flops 1 | bytes 1 | tf_op jit(solution)/shard_map/pallas_call | solution.py:123
  4.1 5.8 %all-to-all-start.1 = ((f32[16,512,128]{2,1,0:T(8,128)}), f32[16,512,128]{2,1,0:T(8,128)}, u32[]{:S(2)}, u32[]{:S(2)}) async-start(f32[16,512,128]{2,1,0:T(8,128)} %bitcast.13), calls=%async_computation.1 | async-start | bytes 8388608 | tf_op jit(solution)/shard_map/all_to_all | solution.py:288
  9.9 5.5 %shard_map.37 = f32[4,4,8,8,8,128]{5,4,3,2,1,0:T(8,128)} custom-call(f32[2,16,4,32,256]{4,3,2,1,0:T(8,128)} %bitcast.16), custom_call_target="tpu_custom_call" | custom-call | flops 1 | bytes 1 | tf_op jit(solution)/shard_map/pallas_call | solution.py:184
  15.4 47.0 %all-to-all-done.1 = f32[16,512,128]{2,1,0:T(8,128)} async-done(((f32[16,512,128]{2,1,0:T(8,128)}), f32[16,512,128]{2,1,0:T(8,128)}, u32[]{:S(2)}, u32[]{:S(2)}) %all-to-all-start.1) | async-done | bytes 4194336 | tf_op jit(solution)/shard_map/all_to_all | solution.py:288
  62.4 0.0 copy-start
  62.4 16.7 %all-to-all-start = ((f32[128,64,128]{2,1,0:T(8,128)}), f32[128,64,128]{2,1,0:T(8,128)}, u32[]{:S(2)}, u32[]{:S(2)}) async-start(f32[128,64,128]{2,1,0:T(8,128)} %bitcast.12), calls=%async_computation | async-start | bytes 8388608 | tf_op jit(solution)/shard_map/all_to_all | solution.py:290
  79.0 0.0 copy-done
  79.0 0.1 broadcast_in_dim.11
  79.1 0.1 broadcast_in_dim.13
  79.3 0.7 reshape_reshape.6.lesser_ref
  79.9 0.9 reshape_reshape.8.result_ref
  80.8 0.2 copy.4
  81.1 0.7 reshape.41.greater_ref
  81.8 7.8 %shard_map.39 = (bf16[512,1024]{1,0:T(8,128)(2,1)}, bf16[512,1024]{1,0:T(8,128)(2,1)}, bf16[512,1024]{1,0:T(8,128)(2,1)}) custom-call(s32[1,512]{1,0:T(1,128)} %reshape_reshape.6.lesser_ref, s32[1,512]{1,0:T(1,128)} %reshape.41.greater_ref, s32[512,1]{1,0:T(8,128)} %reshape_reshape.8.result_ref), custom_call_target="tpu_custom_call" | custom-call | flops 1 | bytes 1 | tf_op jit(solution)/shard_map/pallas_call | solution.py:66
  89.6 9.5 %shard_map.40.l_ref = f32[2,4,512,256]{3,2,1,0:T(8,128)} custom-call(f32[16,2,256,128]{3,2,1,0:T(8,128)} %bitcast.5.x_ref, bf16[512,1024]{1,0:T(8,128)(2,1)} %get-tuple-element.8.table_ref), custom_call_target="tpu_custom_call" | custom-call | flops 1 | bytes 1 | tf_op jit(solution)/shard_map/pallas_call | solution.py:228
  99.1 31.6 %all-to-all-done = f32[128,64,128]{2,1,0:T(8,128)} async-done(((f32[128,64,128]{2,1,0:T(8,128)}), f32[128,64,128]{2,1,0:T(8,128)}, u32[]{:S(2)}, u32[]{:S(2)}) %all-to-all-start) | async-done | bytes 4194336 | tf_op jit(solution)/shard_map/all_to_all | solution.py:290
  130.6 21.4 %shard_map.41 = f32[16,2,256,128]{3,2,1,0:T(8,128)} custom-call(f32[16,8,8,8,128]{4,3,2,1,0:T(8,128)} %bitcast.2.x_ref, f32[2,4,512,256]{3,2,1,0:T(8,128)} %shard_map.40.l_ref, bf16[512,1024]{1,0:T(8,128)(2,1)} %get-tuple-element.9.mirrored_ref, bf16[512,1024]{1,0:T(8,128)(2,1)} %get-tuple-element.10.backward_ref), custom_call_target="tpu_custom_call" | custom-call | flops 1 | bytes 1 | tf_op jit(solution)/shard_map/pallas_call | solution.py:268
  152.1 56.3 %all_to_all.15 = f32[16,512,128]{2,1,0:T(8,128)} all-to-all(f32[16,512,128]{2,1,0:T(8,128)} %bitcast.11), channel_id=1, replica_groups=mesh['mom'=16,'tm'=8] {'mom'}, dimensions={0} | all-to-all | bytes 8388608 | tf_op jit(solution)/shard_map/all_to_all | solution.py:294
  208.4 4.3 %shard_map.42 = f32[2,16,4,32,256]{4,3,2,1,0:T(8,128)} custom-call(f32[16,2,2,16,8,128]{5,4,3,2,1,0:T(8,128)} %bitcast.14), custom_call_target="tpu_custom_call" | custom-call | flops 1 | bytes 1 | tf_op jit(solution)/shard_map/pallas_call | solution.py:146
  (2 shorter events, 0.0 us)
Async XLA Ops:
  4.1 58.3 %all-to-all-start.1 = ((f32[16,512,128]{2,1,0:T(8,128)}), f32[16,512,128]{2,1,0:T(8,128)}, u32[]{:S(2)}, u32[]{:S(2)}) async-start(f32[16,512,128]{2,1,0:T(8,128)} %bitcast.13), calls=%async_computation.1 | async-start | bytes 8388608 | tf_op jit(solution)/shard_map/all_to_all | solution.py:288
  62.4 16.7 %copy-start = (s32[256]{0:T(256)S(1)}, s32[256]{0:T(256)}, u32[]{:S(2)}) copy-start(s32[256]{0:T(256)} %param.5) | copy-start | bytes 3076
  62.4 68.3 %all-to-all-start = ((f32[128,64,128]{2,1,0:T(8,128)}), f32[128,64,128]{2,1,0:T(8,128)}, u32[]{:S(2)}, u32[]{:S(2)}) async-start(f32[128,64,128]{2,1,0:T(8,128)} %bitcast.12), calls=%async_computation | async-start | bytes 8388608 | tf_op jit(solution)/shard_map/all_to_all | solution.py:290

commit v3 on v2

--- a/solution.py
+++ b/solution.py
@@ -1,3 +1,4 @@
+import functools
 import math
 
 import jax
@@ -14,6 +15,8 @@
 BLOCK = (2, 16, 8, 128)
 ANY = pl.BlockSpec(memory_space=pl.ANY)
 HBM = pl.BlockSpec(memory_space=pltpu.HBM)
+SCALAR = pl.BlockSpec(memory_space=pltpu.SMEM)
+DISTANCES = [(dz, dx, dc) for dz in range(2) for dx in range(4) for dc in range(2)]
 
 
 def params():
@@ -108,50 +111,134 @@
 ]
 
 
-def pack_body(i_ref, o_ref, buffer, one, two):
+def shard_at(me, dz, dx, dc, way):
+    x, z, c = me // 4, (me // 2) % 2, me % 2
+    return ((x + way * dx + 4) % 4) * 4 + (z + dz) % 2 * 2 + (c + dc) % 2
+
+
+def moved(values, dz, dx, dc):
+    ways = [(m, (m // 4 + dx) % 4 * 4 + (m // 2 + dz) % 2 * 2 + (m + dc) % 2) for m in range(16)]
+    return lax.ppermute(values, "mom", ways)
+
+
+def pack_body(me_ref, after_ref, i_ref, *refs):
+    near, far = refs[:2], refs[2:6]
+    buffer, one, two = refs[6:]
+    copy = pltpu.make_async_copy
+    loads, stores = [], []
+    for i, (dz, dx, dc) in enumerate(DISTANCES):
+        source = part(i_ref, shard_at(me_ref[0], dz, dx, dc, 1))
+        loads.append([copy(source, buffer.at[i], one.at[i])])
+        stores.append(
+            [
+                copy(half(buffer, i, 0), near[dz].at[dx, dc], two.at[i, 0]),
+                copy(half(buffer, i, 1), far[dx].at[dz, dc], two.at[i, 1]),
+            ]
+        )
+    relay(loads, stores)
+
+
+def pack(me, after, values):
+    return pl.pallas_call(
+        pack_body,
+        in_specs=[SCALAR, HBM, HBM],
+        out_specs=(HBM,) * 6,
+        out_shape=(shape(4, 2, *BLOCK),) * 2 + (shape(2, 2, *BLOCK),) * 4,
+        scratch_shapes=RELAY,
+        compiler_params=params(),
+        cost_estimate=cost(),
+    )(me, after, values)
+
+
+def gather(outs, arrays, ready):
+    pairs = [(i, j, source) for i, blocks in enumerate(outs) for j, source in enumerate(blocks)]
+
+    def body(*refs):
+        made, (buffer, sems) = refs[-2 - len(outs) : -2], refs[-2:]
+        copy = pltpu.make_async_copy
+        relay(
+            [
+                [copy(refs[n].at[index], buffer.at[k], sems.at[0, k])]
+                for k, (_, _, (n, index)) in enumerate(pairs)
+            ],
+            [
+                [copy(buffer.at[k], made[i].at[j], sems.at[1, k])]
+                for k, (i, j, _) in enumerate(pairs)
+            ],
+        )
+
+    return pl.pallas_call(
+        body,
+        in_specs=[HBM] * (len(arrays) + len(ready)),
+        out_specs=(HBM,) * len(outs),
+        out_shape=tuple(shape(len(blocks), *BLOCK) for blocks in outs),
+        scratch_shapes=[
+            pltpu.VMEM((len(pairs), *BLOCK), F32),
+            pltpu.SemaphoreType.DMA((2, len(pairs))),
+        ],
+        compiler_params=params(),
+        cost_estimate=cost(),
+    )(*arrays, *ready)
+
+
+def exchange(sent, ready, between):
+    near = [sent[0], moved(sent[1], 1, 0, 0)]
+    far = [sent[2]] + [moved(sent[2 + dx], 0, dx, 0) for dx in range(1, 4)]
+    over_z = [[(2 + dx, (1, dc)) for dx in range(4)] for dc in range(2)]
+    over_x = [[(dz, (dx, dc)) for dz in range(2) for dc in range(2)] for dx in range(1, 4)]
+    turned = gather([*over_z, *over_x], [*near, *far], ready)
+    ways = [(1, 0, 0), (1, 0, 1), (0, 1, 0), (0, 2, 0), (0, 3, 0)]
+    last = [moved(values, *way) for values, way in zip(turned, ways)]
+    near += last[2:5]
+    over_core = [
+        (1 + dx, 2 * dz + 1) if dx else (dz, (0, 1)) for dz in range(2) for dx in range(4)
+    ]
+    disp = between(turned[0])
+    (beside,) = gather([[(dx, (0, 1)) for dx in range(4)]], far, [disp])
+    far = far + last[:2] + [moved(beside, 0, 0, 1)]
+    (crossing,) = gather([over_core], near, [disp])
+    near.append(moved(crossing, 0, 0, 1))
+    return near, far + [crossing], disp
+
+
+def arrived(refs, h, dz, dx, dc):
+    if h == 0:
+        if dc:
+            return refs[5].at[4 * dz + dx]
+        return refs[1 + dx].at[2 * dz] if dx else refs[dz].at[0, 0]
+    if dz:
+        return refs[4 + dc].at[dx]
+    return refs[6].at[dx] if dc else refs[dx].at[0, 0]
+
+
+def unpack_body(*refs):
+    i_ref, (o_ref, buffer, one, two) = refs[0], refs[-4:]
+    h = 6 - len(refs)
     copy = pltpu.make_async_copy
     relay(
-        [[copy(part(i_ref, m), buffer.at[m], one.at[m])] for m in range(16)],
+        [[copy(i_ref.at[m], buffer.at[m], one.at[m])] for m in range(16)],
         [
-            [copy(half(buffer, m, h), o_ref.at[m, h], two.at[m, h]) for h in range(2)]
+            [copy(buffer.at[m], part(o_ref, m).at[:, :, :, pl.ds(128 * h, 128)], two.at[m])]
             for m in range(16)
         ],
     )
 
 
-def pack(values):
-    return pl.pallas_call(
-        pack_body,
-        in_specs=[HBM],
-        out_specs=HBM,
-        out_shape=shape(16, 2, *BLOCK),
-        scratch_shapes=RELAY,
-        compiler_params=params(),
-        cost_estimate=cost(),
-    )(values)
-
-
-def unpack_body(i_ref, o_ref, buffer, one, two):
-    copy = pltpu.make_async_copy
-    relay(
-        [
-            [copy(i_ref.at[m, h], half(buffer, m, h), two.at[m, h]) for h in range(2)]
-            for m in range(16)
-        ],
-        [[copy(buffer.at[m], part(o_ref, m), one.at[m])] for m in range(16)],
-    )
-
-
-def unpack(values):
+def unpack(values, *done):
     return pl.pallas_call(
         unpack_body,
-        in_specs=[ANY],
+        in_specs=[ANY] + [HBM] * len(done),
         out_specs=HBM,
         out_shape=shape(2, 16, 4, 32, 256),
-        scratch_shapes=RELAY,
-        compiler_params=params(),
-        cost_estimate=cost(),
-    )(values)
+        scratch_shapes=[
+            pltpu.VMEM((16, *BLOCK), F32),
+            pltpu.SemaphoreType.DMA((16,)),
+            pltpu.SemaphoreType.DMA((16,)),
+        ],
+        input_output_aliases={1: 0} if done else {},
+        compiler_params=params(),
+        cost_estimate=cost(),
+    )(values, *done)
 
 
 def swap_rows(tiles):
@@ -217,23 +304,24 @@
 TABLE = pl.BlockSpec((512, 1024), lambda h, t: (0, 0))
 
 
-def lesser_body(x_ref, table_ref, o_ref):
-    step = pl.program_id(1)
-    rows = x_ref.reshape(4096, 128)
-    x = jnp.concatenate([rows[pl.ds(2 * step + i, 512, stride=8), :] for i in range(2)], 1)
-    o_ref[0, 0] = times(table_ref, x)
-
-
-def lesser_transform(rows, table):
-    return pl.pallas_call(
-        lesser_body,
+def greater_body(after_ref, x_ref, table_ref, o_ref):
+    pairs = []
+    for i in range(2):
+        tiles = [x_ref[:, s, i].reshape(128, 128) for s in range(4)]
+        pairs.append(jnp.concatenate(swap_blocks(tiles), 0))
+    o_ref[0, 0] = times(table_ref, jnp.concatenate(pairs, 1))
+
+
+def greater_transform(after, rows, table):
+    return pl.pallas_call(
+        greater_body,
         grid=(2, 4),
-        in_specs=[ROWS, TABLE],
+        in_specs=[HBM, pl.BlockSpec((16, 4, 2, 8, 128), lambda h, t: (0, h, t, 0, 0)), TABLE],
         out_specs=DISP,
         out_shape=shape(2, 4, 512, 256),
         compiler_params=params(),
         cost_estimate=cost(),
-    )(rows, table)
+    )(after, rows, table)
 
 
 def bubble(lesser, greater):
@@ -242,14 +330,28 @@
     return jnp.concatenate([lr * gi + li * gr, li * gi - lr * gr], 0)
 
 
-def bubble_body(x_ref, l_ref, mirrored_ref, backward_ref, o_ref, result_ref):
-    step = pl.program_id(1)
-    pairs = []
-    for i in range(2):
-        tiles = [x_ref[:, s, i].reshape(128, 128) for s in range(4)]
-        pairs.append(jnp.concatenate(swap_blocks(tiles), 0))
-    product = bubble(l_ref[0, 0], times(mirrored_ref, jnp.concatenate(pairs, 1)))
-    result = times(backward_ref, product)
+def bubble_body(h, me_ref, g_ref, forward_ref, backward_ref, *refs):
+    held, (o_ref, rows_ref, result_ref, sems) = refs[:-4], refs[-4:]
+    step = pl.program_id(0)
+
+    @pl.when(step == 0)
+    def _():
+        copies = [
+            pltpu.make_async_copy(
+                arrived(held, h, dz, dx, dc),
+                rows_ref.at[shard_at(me_ref[0], dz, dx, dc, -1)],
+                sems.at[i],
+            )
+            for i, (dz, dx, dc) in enumerate(DISTANCES)
+        ]
+        for copy in copies:
+            copy.start()
+        for copy in copies:
+            copy.wait()
+
+    rows = rows_ref.reshape(4096, 128)
+    x = jnp.concatenate([rows[pl.ds(2 * step + i, 512, stride=8), :] for i in range(2)], 1)
+    result = times(backward_ref, bubble(times(forward_ref, x), g_ref[0, 0]))
     for i in range(2):
         result_ref[2 * step + i] = result[:, 128 * i : 128 * i + 128]
 
@@ -258,41 +360,48 @@
         def shard(m, carry):
             row = pl.multiple_of(32 * m, 32)
             tiles = [result_ref[t, pl.ds(row, 32), :].reshape(4, 8, 128) for t in range(8)]
-            o_ref[m, 0] = jnp.stack(swap_rows(tiles), 1).reshape(256, 128)
+            o_ref[m] = jnp.stack(swap_rows(tiles), 1).reshape(256, 128)
             return carry
 
         lax.fori_loop(0, 16, shard, 0)
 
 
-def bubble_transform(greater, lesser_disp, mirrored, backward):
-    return pl.pallas_call(
-        bubble_body,
-        grid=(2, 4),
-        in_specs=[
-            pl.BlockSpec((16, 4, 2, 8, 128), lambda h, t: (0, h, t, 0, 0)),
-            DISP,
-            TABLE,
-            TABLE,
+def bubble_transform(h, me, held, greater_disp, forward, backward):
+    table = pl.BlockSpec((512, 1024), lambda t: (0, 0))
+    return pl.pallas_call(
+        functools.partial(bubble_body, h),
+        grid=(4,),
+        in_specs=[SCALAR, pl.BlockSpec((1, 1, 512, 256), lambda t: (h, t, 0, 0)), table, table]
+        + [HBM] * len(held),
+        out_specs=pl.BlockSpec((16, 256, 128), lambda t: (0, 0, 0)),
+        out_shape=shape(16, 256, 128),
+        scratch_shapes=[
+            pltpu.VMEM((16, *BLOCK), F32),
+            pltpu.VMEM((8, 512, 128), F32),
+            pltpu.SemaphoreType.DMA((16,)),
         ],
-        out_specs=ROWS,
-        out_shape=shape(16, 2, 256, 128),
-        scratch_shapes=[pltpu.VMEM((8, 512, 128), F32)],
-        compiler_params=params(),
-        cost_estimate=cost(),
-    )(greater, lesser_disp, mirrored, backward)
+        compiler_params=params(),
+        cost_estimate=cost(),
+    )(me, greater_disp, forward, backward, *held)
 
 
 def local(lesser, greater, site_of):
     merged = (2, 16, 4, 32, 256)
-    lesser_out = pack(lesser.reshape(merged)).reshape(16, 512, 128)
-    lesser_rows = lax.all_to_all(lesser_out, "mom", 0, 0, tiled=True).reshape(16, 2, 256, 128)
-    greater_out = pack_greater(greater.reshape(merged)).reshape(128, 64, 128)
-    greater_rows = lax.all_to_all(greater_out, ("mom", "tm"), 0, 0, tiled=True)
+    me = lax.axis_index("mom").reshape(1)
+    greater_out = pack_greater(greater.reshape(merged))
+    greater_rows = lax.all_to_all(
+        greater_out.reshape(128, 64, 128), ("mom", "tm"), 0, 0, tiled=True
+    ).reshape(16, 8, 8, 8, 128)
+    sent = pack(me, greater_out, lesser.reshape(merged))
     forward, mirrored, backward = phase_tables(site_of)
-    disp = lesser_transform(lesser_rows, forward)
-    moved = bubble_transform(greater_rows.reshape(16, 8, 8, 8, 128), disp, mirrored, backward)
-    back = lax.all_to_all(moved.reshape(16, 512, 128), "mom", 0, 0, tiled=True)
-    return unpack(back.reshape(16, 2, *BLOCK)).reshape(lesser.shape)
+    near, far, disp = exchange(
+        sent, (forward,), lambda turned: greater_transform(turned, greater_rows, mirrored)
+    )
+    far = bubble_transform(1, me, far, disp, forward, backward)
+    far = lax.all_to_all(far, "mom", 0, 0, tiled=True).reshape(16, *BLOCK)
+    near = bubble_transform(0, me, near, disp, forward, backward)
+    near = lax.all_to_all(near, "mom", 0, 0, tiled=True).reshape(16, *BLOCK)
+    return unpack(near, unpack(far)).reshape(lesser.shape)
 
 
 def solution(mesh):

time: 214 us -> 207 us (0.967); the launches traced: 213 us -> 203 us
  blocking collectives: 56.3 us -> 0 us
  waiting for transfers between devices: 78.5 us -> 93.9 us
  Pallas kernels: 52.5 us -> 66.1 us
  starting transfers between devices: 22.5 us -> 35.5 us
  local copies, waits for them, and re-layouts: 2.75 us -> 7.53 us
    ppermute x0 -> x11, waiting for transfers between devices: none -> 57.9 us  [moved(): return lax.ppermute(values, 'mom', ways)]
    all_to_all x1 -> x0, blocking collectives: 56.3 us -> none  [local(): back = lax.all_to_all(moved.reshape(16, 512, 128), 'mom', 0, 0, tiled=True)]
    all_to_all x2 -> x3, waiting for transfers between devices: 78.5 us -> 36 us  [the longest x1 25.2 us: local(): near = lax.all_to_all(near, 'mom', 0, 0, tiled=True).reshape(16, *BLOCK)]
    ppermute x0 -> x11, starting transfers between devices: none -> 15.1 us  [moved(): return lax.ppermute(values, 'mom', ways)]
    pallas_call x4 -> x9, Pallas kernels: 39.3 us -> 52.9 us  [the longest x2 26.2 us: bubble_transform(): pl.pallas_call(functools.partial(bubble_body, h), grid=(4,), in_specs=[SC...]
    unnamed x2 -> x30, local copies, waits for them, and re-layouts: 0.01 us -> 4.89 us
    all_to_all x2 -> x3, starting transfers between devices: 22.5 us -> 20.4 us  [the longest x1 10.7 us: local(): lax.all_to_all(greater_out.reshape(128, 64, 128), ('mom', 'tm'), 0, 0, ti...]
  transfers between devices with their start and end apart: 2 -> 14, of which waited for: 2 -> 8; matrix products, arithmetic and copies ran while one was open for 1% -> 1% of each run, Pallas kernels for 11% -> 22%
where the time goes in v3:
time: 207 us; the launch traced here: 203 us
  waiting for transfers between devices  93.9 us (45%)
  Pallas kernels  66.1 us (32%)
  starting transfers between devices  35.5 us (17%)
  local copies, waits for them, and re-layouts  7.53 us (4%)
    ppermute x11, waiting for transfers between devices, moved(): return lax.ppermute(values, 'mom', ways)  57.9 us
    pallas_call x2, Pallas kernels, bubble_transform(): pl.pallas_call(functools.partial(bubble_body, h), grid=(4,), in_specs=[SC...  26.2 us
    all_to_all x1, waiting for transfers between devices, local(): near = lax.all_to_all(near, 'mom', 0, 0, tiled=True).reshape(16, *BLOCK)  25.2 us
    ppermute x11, starting transfers between devices, moved(): return lax.ppermute(values, 'mom', ways)  15.1 us
    all_to_all x1, waiting for transfers between devices, local(): far = lax.all_to_all(far, 'mom', 0, 0, tiled=True).reshape(16, *BLOCK)  10.9 us
    all_to_all x1, starting transfers between devices, local(): lax.all_to_all(greater_out.reshape(128, 64, 128), ('mom', 'tm'), 0, 0, ti...  10.7 us
    pallas_call x1, Pallas kernels, greater_transform(): pl.pallas_call(greater_body, grid=(2, 4), in_specs=[HBM, pl.BlockSpec((16...  10.6 us
    pallas_call x1, Pallas kernels, phase_tables(): pl.pallas_call(table_body, out_shape=(jax.ShapeDtypeStruct((512, 1024), B...  7.72 us
  transfers between devices with their start and end apart: 14, of which 8 were waited for; matrix products, arithmetic and copies ran while one was open for 1% of the time, Pallas kernels for 22%

profile of v3, /device:TPU:24, one launch (start us, length us, event | category | flops | bytes accessed | tf_op | source)
XLA Modules:
  0.0 203.4 jit_solution(3886282158405453732)
XLA Ops:
  0.0 5.4 %shard_map.37.after_ref = f32[4,4,8,8,8,128]{5,4,3,2,1,0:T(8,128)} custom-call(f32[2,16,4,32,256]{4,3,2,1,0:T(8,128)} %bitcast.12), custom_call_target="tpu_custom_call" | custom-call | flops 1 | bytes 1 | tf_op jit(solution)/shard_map/pallas_call | solution.py:271
  5.5 10.7 %all-to-all-start = ((f32[128,64,128]{2,1,0:T(8,128)}), f32[128,64,128]{2,1,0:T(8,128)}, u32[]{:S(2)}, u32[]{:S(2)}) async-start(f32[128,64,128]{2,1,0:T(8,128)} %bitcast.10), calls=%async_computation | async-start | bytes 8388608 | tf_op jit(solution)/shard_map/all_to_all | solution.py:392
  16.2 4.2 %shard_map.38 = (f32[4,2,2,16,8,128]{5,4,3,2,1,0:T(8,128)}, f32[4,2,2,16,8,128]{5,4,3,2,1,0:T(8,128)}, f32[2,2,2,16,8,128]{5,4,3,2,1,0:T(8,128)}, f32[2,2,2,16,8...) custom-call(s32[1]{0:T(128)} %bitcast.me_ref, ...), custom_call_target="tpu_custom_call" | custom-call | flops 1 | bytes 1 | tf_op jit(solution)/shard_map/pallas_call | solution.py:142
  20.4 1.8 collective-permute-start
  22.2 1.5 collective-permute-start.1
  23.7 2.7 %collective-permute-start.2 = (f32[2,2,2,16,8,128]{5,4,3,2,1,0:T(8,128)}, f32[2,2,2,16,8,128]{5,4,3,2,1,0:T(8,128)S(1)}, u32[]{:S(2)}, u32[]{:S(2)}) collective-permute-start(f32[2,2,2,16,8,128]{5,4,3,2,1,0:T(8,128)} %get-tuple-element.23), channel_id=1, source_target_pairs={{0,64},{8,72},{16,80},{24,88},{32,96},{40,104},{48,112},{56,120},{... | collective-permute-start | bytes 1572872 | tf_op jit(solution)/shard_map/ppermute | solution.py:121
  26.4 1.4 collective-permute-start.3
  28.7 0.9 reshape_reshape.8.result_ref
  30.5 7.7 %shard_map.39 = (bf16[512,1024]{1,0:T(8,128)(2,1)}, bf16[512,1024]{1,0:T(8,128)(2,1)}, bf16[512,1024]{1,0:T(8,128)(2,1)}) custom-call(s32[1,512]{1,0:T(1,128)} %reshape_reshape.6.lesser_ref, s32[1,512]{1,0:T(1,128)} %reshape.35.greater_ref, s32[512,1]{1,0:T(8,128)} %reshape_reshape.8.result_ref), custom_call_target="tpu_custom_call" | custom-call | flops 1 | bytes 1 | tf_op jit(solution)/shard_map/pallas_call | solution.py:69
  38.2 36.9 %collective-permute-done.1.refs_3_.refs_1_ = f32[2,2,2,16,8,128]{5,4,3,2,1,0:T(8,128)S(1)} collective-permute-done((f32[2,2,2,16,8,128]{5,4,3,2,1,0:T(8,128)}, f32[2,2,2,16,8,128]{5,4,3,2,1,0:T(8,128)S(1)}, u32[]{:S(2)}, u32[]{:S(2)}) %collective-permute-start.1) | collective-permute-done | bytes 524320 | tf_op jit(solution)/shard_map/ppermute | solution.py:121
  75.2 11.3 %collective-permute-done.2.refs_4_.refs_2_ = f32[2,2,2,16,8,128]{5,4,3,2,1,0:T(8,128)S(1)} collective-permute-done((f32[2,2,2,16,8,128]{5,4,3,2,1,0:T(8,128)}, f32[2,2,2,16,8,128]{5,4,3,2,1,0:T(8,128)S(1)}, u32[]{:S(2)}, u32[]{:S(2)}) %collective-permute-start.2) | collective-permute-done | bytes 524320 | tf_op jit(solution)/shard_map/ppermute | solution.py:121
  86.5 0.8 copy-done.3
  87.9 2.9 %shard_map.40 = (f32[4,2,16,8,128]{4,3,2,1,0:T(8,128)}, f32[4,2,16,8,128]{4,3,2,1,0:T(8,128)}, f32[4,2,16,8,128]{4,3,2,1,0:T(8,128)}, f32[4,2,16,8,128]{4,3,2,1,0:T(8,128)}, f32[4,2,16,8,128]{4,3,2,1,0:T(8,128)}) custom-call(f32[4,2,2,16,8,128]{5,4,3,2,1,0:T(8,128)} %get-tuple-element.19.refs_0_, f32[4,2,2,16,8,128]{5,4,3,2,1,0:T(8,128)} %copy-done, ...), custom_call_target="tpu_custom_call" | custom-call | flops 1 | bytes 1 | tf_op jit(solution)/shard_map/pallas_call | solution.py:170
  91.5 2.4 %collective-permute-start.5 = (f32[4,2,16,8,128]{4,3,2,1,0:T(8,128)}, f32[4,2,16,8,128]{4,3,2,1,0:T(8,128)S(1)}, u32[]{:S(2)}, u32[]{:S(2)}) collective-permute-start(f32[4,2,16,8,128]{4,3,2,1,0:T(8,128)} %get-tuple-element.30), channel_id=1, source_target_pairs={{0,64},{8,72},{16,80},{24,88},{32,96},{40,104},{48,112},{56,120},{... | collective-permute-start | bytes 1572872 | tf_op jit(solution)/shard_map/ppermute | solution.py:121
  93.9 1.9 collective-permute-start.6
  96.3 10.6 %shard_map.41.refs_5_.g_ref.refs_4_ = f32[2,4,512,256]{3,2,1,0:T(8,128)} custom-call(f32[4,2,16,8,128]{4,3,2,1,0:T(8,128)} %get-tuple-element.26.after_ref, f32[16,8,8,8,128]{4,3,2,1,0:T(8,128)} %bitcast.5.x_ref, bf16[512,1024]{1,0:T(8,128)(2,1)} %get-tuple-element.27.table_ref), custom_call_target="tpu_custom_call" | custom-call | flops 1 | bytes 1 | tf_op jit(solution)/shard_map/pallas_call | solution.py:316
  106.9 1.8 shard_map.44
  108.8 1.6 collective-permute-start.10
  110.4 6.8 %collective-permute-done.5.refs_3_ = f32[4,2,16,8,128]{4,3,2,1,0:T(8,128)S(1)} collective-permute-done((f32[4,2,16,8,128]{4,3,2,1,0:T(8,128)}, f32[4,2,16,8,128]{4,3,2,1,0:T(8,128)S(1)}, u32[]{:S(2)}, u32[]{:S(2)}) %collective-permute-start.5) | collective-permute-done | bytes 524320 | tf_op jit(solution)/shard_map/ppermute | solution.py:121
  118.1 0.8 copy-done.8
  118.9 2.1 %shard_map.42.refs_7_ = f32[8,2,16,8,128]{4,3,2,1,0:T(8,128)} custom-call(f32[4,2,2,16,8,128]{5,4,3,2,1,0:T(8,128)} %get-tuple-element.19.refs_0_, f32[4,2,2,16,8,128]{5,4,3,2,1,0:T(8,128)} %copy-done, f32[4,2,16,8,128]{4,3,2,1,0:T(8,128)} %copy-done.6, f32[4,2,16,8,128]{4,3,2,1,0:T(8,128)} %copy-done.7, f32[4,2,16,8,128]{4,3,2,1,0:T(8,128)} %copy-done.8, ...), custom_call_target="tpu_custom_call" | custom-call | flops 1 | bytes 1 | tf_op jit(solution)/shard_map/pallas_call | solution.py:170
  121.1 0.8 copy-done.11
  122.3 13.1 %shard_map.45 = f32[16,256,128]{2,1,0:T(8,128)} custom-call(s32[1]{0:T(128)} %bitcast.me_ref, f32[2,4,512,256]{3,2,1,0:T(8,128)} %shard_map.41.refs_5_.g_ref.refs_4_, bf16[512,1024]{1,0:T(8,128)(2,1)} %get-tuple-element.25.refs_6_.forward_ref, bf16[512,1024]{1,0:T(8,128)(2,1)} %get-tuple-element.28.backward_ref, ...), custom_call_target="tpu_custom_call" | custom-call | flops 1 | bytes 1 | tf_op jit(solution)/shard_map/pallas_call | solution.py:371
  135.4 4.8 %all-to-all-start.2 = ((f32[16,256,128]{2,1,0:T(8,128)}), f32[16,256,128]{2,1,0:T(8,128)S(1)}, u32[]{:S(2)}, u32[]{:S(2)}) async-start(f32[16,256,128]{2,1,0:T(8,128)} %shard_map.45), calls=%async_computation.2 | async-start | bytes 4194304 | tf_op jit(solution)/shard_map/all_to_all | solution.py:401
  140.7 2.3 %collective-permute-done.7.refs_5_ = f32[8,2,16,8,128]{4,3,2,1,0:T(8,128)S(1)} collective-permute-done((f32[8,2,16,8,128]{4,3,2,1,0:T(8,128)S(1)}, f32[8,2,16,8,128]{4,3,2,1,0:T(8,128)S(1)}, u32[]{:S(2)}, u32[]{:S(2)}) %collective-permute-start.7) | collective-permute-done | bytes 1048608 | tf_op jit(solution)/shard_map/ppermute | solution.py:121
  143.0 1.0 copy-done.9
  144.0 13.1 %shard_map.43 = f32[16,256,128]{2,1,0:T(8,128)} custom-call(s32[1]{0:T(128)} %bitcast.me_ref, f32[2,4,512,256]{3,2,1,0:T(8,128)} %shard_map.41.refs_5_.g_ref.refs_4_, bf16[512,1024]{1,0:T(8,128)(2,1)} %get-tuple-element.25.refs_6_.forward_ref, bf16[512,1024]{1,0:T(8,128)(2,1)} %get-tuple-element.28.backward_ref, ...), custom_call_target="tpu_custom_call" | custom-call | flops 1 | bytes 1 | tf_op jit(solution)/shard_map/pallas_call | solution.py:371
  157.1 10.9 %all-to-all-done.2 = f32[16,256,128]{2,1,0:T(8,128)S(1)} async-done(((f32[16,256,128]{2,1,0:T(8,128)}), f32[16,256,128]{2,1,0:T(8,128)S(1)}, u32[]{:S(2)}, u32[]{:S(2)}) %all-to-all-start.2) | async-done | bytes 2097184 | tf_op jit(solution)/shard_map/all_to_all | solution.py:401
  168.0 4.9 %all-to-all-start.1 = ((f32[16,256,128]{2,1,0:T(8,128)}), f32[16,256,128]{2,1,0:T(8,128)}, u32[]{:S(2)}, u32[]{:S(2)}) async-start(f32[16,256,128]{2,1,0:T(8,128)} %shard_map.43), calls=%async_computation.1 | async-start | bytes 4194304 | tf_op jit(solution)/shard_map/all_to_all | solution.py:403
  172.9 2.6 %shard_map.46.refs_1_ = f32[2,16,4,32,256]{4,3,2,1,0:T(8,128)} custom-call(f32[16,2,16,8,128]{4,3,2,1,0:T(8,128)} %bitcast.11), custom_call_target="tpu_custom_call" | custom-call | flops 1 | bytes 1 | tf_op jit(solution)/shard_map/pallas_call | solution.py:228
  175.5 25.2 %all-to-all-done.1 = f32[16,256,128]{2,1,0:T(8,128)} async-done(((f32[16,256,128]{2,1,0:T(8,128)}), f32[16,256,128]{2,1,0:T(8,128)}, u32[]{:S(2)}, u32[]{:S(2)}) %all-to-all-start.1) | async-done | bytes 2097184 | tf_op jit(solution)/shard_map/all_to_all | solution.py:403
  200.7 2.6 %shard_map.47 = f32[2,16,4,32,256]{4,3,2,1,0:T(8,128)} custom-call(f32[16,2,16,8,128]{4,3,2,1,0:T(8,128)} %bitcast.6.refs_0_, f32[2,16,4,32,256]{4,3,2,1,0:T(8,128)} %shard_map.46.refs_1_), custom_call_target="tpu_custom_call", output_to_operand_aliasing={{}: (1, {})} | custom-call | flops 1 | bytes 1 | tf_op jit(solution)/shard_map/pallas_call | solution.py:228
  (45 shorter events, 5.5 us)
Async XLA Ops:
  5.5 90.9 %all-to-all-start = ((f32[128,64,128]{2,1,0:T(8,128)}), f32[128,64,128]{2,1,0:T(8,128)}, u32[]{:S(2)}, u32[]{:S(2)}) async-start(f32[128,64,128]{2,1,0:T(8,128)} %bitcast.10), calls=%async_computation | async-start | bytes 8388608 | tf_op jit(solution)/shard_map/all_to_all | solution.py:392
  16.2 11.6 %copy-start.13 = (s32[256]{0:T(256)S(1)}, s32[256]{0:T(256)}, u32[]{:S(2)}) copy-start(s32[256]{0:T(256)} %param.5) | copy-start | bytes 3076
  20.4 66.1 %collective-permute-start = (f32[4,2,2,16,8,128]{5,4,3,2,1,0:T(8,128)}, f32[4,2,2,16,8,128]{5,4,3,2,1,0:T(8,128)S(1)}, u32[]{:S(2)}, u32[]{:S(2)}) collective-permute-start(f32[4,2,2,16,8,128]{5,4,3,2,1,0:T(8,128)} %get-tuple-element.20), channel_id=1, source_target_pairs={{0,16},{8,24},{16,0},{24,8},{32,48},{40,56},{48,32},{56,40},{64,80... | collective-permute-start | bytes 3145736 | tf_op jit(solution)/shard_map/ppermute | solution.py:121
  22.2 53.0 %collective-permute-start.1 = (f32[2,2,2,16,8,128]{5,4,3,2,1,0:T(8,128)}, f32[2,2,2,16,8,128]{5,4,3,2,1,0:T(8,128)S(1)}, u32[]{:S(2)}, u32[]{:S(2)}) collective-permute-start(f32[2,2,2,16,8,128]{5,4,3,2,1,0:T(8,128)} %get-tuple-element.22), channel_id=1, source_target_pairs={{0,32},{8,40},{16,48},{24,56},{32,64},{40,72},{48,80},{56,88},{64,... | collective-permute-start | bytes 1572872 | tf_op jit(solution)/shard_map/ppermute | solution.py:121
  23.7 62.8 %collective-permute-start.2 = (f32[2,2,2,16,8,128]{5,4,3,2,1,0:T(8,128)}, f32[2,2,2,16,8,128]{5,4,3,2,1,0:T(8,128)S(1)}, u32[]{:S(2)}, u32[]{:S(2)}) collective-permute-start(f32[2,2,2,16,8,128]{5,4,3,2,1,0:T(8,128)} %get-tuple-element.23), channel_id=1, source_target_pairs={{0,64},{8,72},{16,80},{24,88},{32,96},{40,104},{48,112},{56,120},{... | collective-permute-start | bytes 1572872 | tf_op jit(solution)/shard_map/ppermute | solution.py:121
  26.4 60.1 %collective-permute-start.3 = (f32[2,2,2,16,8,128]{5,4,3,2,1,0:T(8,128)}, f32[2,2,2,16,8,128]{5,4,3,2,1,0:T(8,128)S(1)}, u32[]{:S(2)}, u32[]{:S(2)}) collective-permute-start(f32[2,2,2,16,8,128]{5,4,3,2,1,0:T(8,128)} %get-tuple-element.24), channel_id=1, source_target_pairs={{0,96},{8,104},{16,112},{24,120},{32,0},{40,8},{48,16},{56,24},{64... | collective-permute-start | bytes 1572872 | tf_op jit(solution)/shard_map/ppermute | solution.py:121
  75.2 11.3 %copy-start.2 = (f32[2,2,2,16,8,128]{5,4,3,2,1,0:T(8,128)}, f32[2,2,2,16,8,128]{5,4,3,2,1,0:T(8,128)S(1)}, u32[]{:S(2)}) copy-start(f32[2,2,2,16,8,128]{5,4,3,2,1,0:T(8,128)S(1)} %collective-permute-done.1.refs_3_.refs_1_) | copy-start | bytes 1572868
  86.5 0.8 copy-start.3
  86.5 1.0 copy-start.4
  86.5 1.4 copy-start
  90.8 17.9 %collective-permute-start.4 = (f32[4,2,16,8,128]{4,3,2,1,0:T(8,128)}, f32[4,2,16,8,128]{4,3,2,1,0:T(8,128)S(1)}, u32[]{:S(2)}, u32[]{:S(2)}) collective-permute-start(f32[4,2,16,8,128]{4,3,2,1,0:T(8,128)} %get-tuple-element.29), channel_id=1, source_target_pairs={{0,32},{8,40},{16,48},{24,56},{32,64},{40,72},{48,80},{56,88},{64,... | collective-permute-start | bytes 1572872 | tf_op jit(solution)/shard_map/ppermute | solution.py:121
  91.5 25.7 %collective-permute-start.5 = (f32[4,2,16,8,128]{4,3,2,1,0:T(8,128)}, f32[4,2,16,8,128]{4,3,2,1,0:T(8,128)S(1)}, u32[]{:S(2)}, u32[]{:S(2)}) collective-permute-start(f32[4,2,16,8,128]{4,3,2,1,0:T(8,128)} %get-tuple-element.30), channel_id=1, source_target_pairs={{0,64},{8,72},{16,80},{24,88},{32,96},{40,104},{48,112},{56,120},{... | collective-permute-start | bytes 1572872 | tf_op jit(solution)/shard_map/ppermute | solution.py:121
  93.9 23.7 %collective-permute-start.6 = (f32[4,2,16,8,128]{4,3,2,1,0:T(8,128)}, f32[4,2,16,8,128]{4,3,2,1,0:T(8,128)S(1)}, u32[]{:S(2)}, u32[]{:S(2)}) collective-permute-start(f32[4,2,16,8,128]{4,3,2,1,0:T(8,128)} %get-tuple-element.31), channel_id=1, source_target_pairs={{0,96},{8,104},{16,112},{24,120},{32,0},{40,8},{48,16},{56,24},{64... | collective-permute-start | bytes 1572872 | tf_op jit(solution)/shard_map/ppermute | solution.py:121
  95.7 25.4 %collective-permute-start.8 = (f32[4,2,16,8,128]{4,3,2,1,0:T(8,128)}, f32[4,2,16,8,128]{4,3,2,1,0:T(8,128)S(1)}, u32[]{:S(2)}, u32[]{:S(2)}) collective-permute-start(f32[4,2,16,8,128]{4,3,2,1,0:T(8,128)} %get-tuple-element.26.after_ref), channel_id=1, source_target_pairs={{0,16},{8,24},{16,0},{24,8},{32,48},{40,56},{48,32},{56,40},{64,80... | collective-permute-start | bytes 1572872 | tf_op jit(solution)/shard_map/ppermute | solution.py:121
  96.3 10.6 %copy-start.14 = (f32[4,2,16,8,128]{4,3,2,1,0:T(8,128)S(1)}, f32[4,2,16,8,128]{4,3,2,1,0:T(8,128)}, u32[]{:S(2)}) copy-start(f32[4,2,16,8,128]{4,3,2,1,0:T(8,128)} %get-tuple-element.32) | copy-start | bytes 1572868
  106.9 14.2 %collective-permute-start.9 = (f32[4,2,16,8,128]{4,3,2,1,0:T(8,128)S(1)}, f32[4,2,16,8,128]{4,3,2,1,0:T(8,128)S(1)}, u32[]{:S(2)}, u32[]{:S(2)}) collective-permute-start(f32[4,2,16,8,128]{4,3,2,1,0:T(8,128)S(1)} %copy-done.14), channel_id=1, source_target_pairs={{0,24},{8,16},{16,8},{24,0},{32,56},{40,48},{48,40},{56,32},{64,88... | collective-permute-start | bytes 1572872 | tf_op jit(solution)/shard_map/ppermute | solution.py:121
  108.7 8.9 %copy-start.6 = (f32[4,2,16,8,128]{4,3,2,1,0:T(8,128)}, f32[4,2,16,8,128]{4,3,2,1,0:T(8,128)S(1)}, u32[]{:S(2)}) copy-start(f32[4,2,16,8,128]{4,3,2,1,0:T(8,128)S(1)} %collective-permute-done.4.refs_2_) | copy-start | bytes 1572868
  108.8 12.4 %collective-permute-start.10 = (f32[4,2,16,8,128]{4,3,2,1,0:T(8,128)}, f32[4,2,16,8,128]{4,3,2,1,0:T(8,128)S(1)}, u32[]{:S(2)}, u32[]{:S(2)}) collective-permute-start(f32[4,2,16,8,128]{4,3,2,1,0:T(8,128)} %shard_map.44), channel_id=1, source_target_pairs={{0,8},{8,0},{16,24},{24,16},{32,40},{40,32},{48,56},{56,48},{64,72... | collective-permute-start | bytes 1572872 | tf_op jit(solution)/shard_map/ppermute | solution.py:121
  117.2 0.8 copy-start.7
  118.0 0.8 copy-start.8
  121.1 0.8 copy-start.11
  121.1 1.0 copy-start.10
  121.1 1.2 copy-start.12
  135.4 4.8 %copy-start.5 = (f32[8,2,16,8,128]{4,3,2,1,0:T(8,128)S(1)}, f32[8,2,16,8,128]{4,3,2,1,0:T(8,128)}, u32[]{:S(2)}) copy-start(f32[8,2,16,8,128]{4,3,2,1,0:T(8,128)} %shard_map.42.refs_7_) | copy-start | bytes 3145732
  135.4 32.6 %all-to-all-start.2 = ((f32[16,256,128]{2,1,0:T(8,128)}), f32[16,256,128]{2,1,0:T(8,128)S(1)}, u32[]{:S(2)}, u32[]{:S(2)}) async-start(f32[16,256,128]{2,1,0:T(8,128)} %shard_map.45), calls=%async_computation.2 | async-start | bytes 4194304 | tf_op jit(solution)/shard_map/all_to_all | solution.py:401
  140.2 2.8 %collective-permute-start.7 = (f32[8,2,16,8,128]{4,3,2,1,0:T(8,128)S(1)}, f32[8,2,16,8,128]{4,3,2,1,0:T(8,128)S(1)}, u32[]{:S(2)}, u32[]{:S(2)}) collective-permute-start(f32[8,2,16,8,128]{4,3,2,1,0:T(8,128)S(1)} %copy-done.5), channel_id=1, source_target_pairs={{0,8},{8,0},{16,24},{24,16},{32,40},{40,32},{48,56},{56,48},{64,72... | collective-permute-start | bytes 3145736 | tf_op jit(solution)/shard_map/ppermute | solution.py:121
  143.0 1.0 copy-start.9
  168.0 4.9 %copy-start.1 = (f32[16,256,128]{2,1,0:T(8,128)}, f32[16,256,128]{2,1,0:T(8,128)S(1)}, u32[]{:S(2)}) copy-start(f32[16,256,128]{2,1,0:T(8,128)S(1)} %all-to-all-done.2) | copy-start | bytes 6291460
  168.0 32.7 %all-to-all-start.1 = ((f32[16,256,128]{2,1,0:T(8,128)}), f32[16,256,128]{2,1,0:T(8,128)}, u32[]{:S(2)}, u32[]{:S(2)}) async-start(f32[16,256,128]{2,1,0:T(8,128)} %shard_map.43), calls=%async_computation.1 | async-start | bytes 4194304 | tf_op jit(solution)/shard_map/all_to_all | solution.py:403

commit v4 on v3

--- a/solution.py
+++ b/solution.py
@@ -77,9 +77,8 @@
 def times(table_ref, x):
     high, low = split(x)
     table_high, table_low = table_ref[:, 0:512], table_ref[:, 512:1024]
-    product = jnp.dot(table_high, high, preferred_element_type=F32)
-    product += jnp.dot(table_high, low, preferred_element_type=F32)
-    return product + jnp.dot(table_low, high, preferred_element_type=F32)
+    tables = jnp.concatenate([table_high, table_high, table_low], 1)
+    return jnp.dot(tables, jnp.concatenate([high, low, high], 0), preferred_element_type=F32)
 
 
 def part(ref, m):
@@ -169,7 +168,7 @@
 
     return pl.pallas_call(
         body,
-        in_specs=[HBM] * (len(arrays) + len(ready)),
+        in_specs=[ANY] * len(arrays) + [HBM] * len(ready),
         out_specs=(HBM,) * len(outs),
         out_shape=tuple(shape(len(blocks), *BLOCK) for blocks in outs),
         scratch_shapes=[
@@ -198,7 +197,7 @@
     far = far + last[:2] + [moved(beside, 0, 0, 1)]
     (crossing,) = gather([over_core], near, [disp])
     near.append(moved(crossing, 0, 0, 1))
-    return near, far + [crossing], disp
+    return near, far, crossing, disp
 
 
 def arrived(refs, h, dz, dx, dc):
@@ -299,26 +298,29 @@
     )
 
 
-ROWS = pl.BlockSpec((16, 1, 256, 128), lambda h, t: (0, h, 0, 0))
-DISP = pl.BlockSpec((1, 1, 512, 256), lambda h, t: (h, t, 0, 0))
-TABLE = pl.BlockSpec((512, 1024), lambda h, t: (0, 0))
+WIDE = 4
 
 
 def greater_body(after_ref, x_ref, table_ref, o_ref):
-    pairs = []
-    for i in range(2):
+    parts = []
+    for i in range(WIDE):
         tiles = [x_ref[:, s, i].reshape(128, 128) for s in range(4)]
-        pairs.append(jnp.concatenate(swap_blocks(tiles), 0))
-    o_ref[0, 0] = times(table_ref, jnp.concatenate(pairs, 1))
+        parts.append(jnp.concatenate(swap_blocks(tiles), 0))
+    o_ref[0, 0] = times(table_ref, jnp.concatenate(parts, 1))
 
 
 def greater_transform(after, rows, table):
+    steps = 8 // WIDE
     return pl.pallas_call(
         greater_body,
-        grid=(2, 4),
-        in_specs=[HBM, pl.BlockSpec((16, 4, 2, 8, 128), lambda h, t: (0, h, t, 0, 0)), TABLE],
-        out_specs=DISP,
-        out_shape=shape(2, 4, 512, 256),
+        grid=(2, steps),
+        in_specs=[
+            HBM,
+            pl.BlockSpec((16, 4, WIDE, 8, 128), lambda h, t: (0, h, t, 0, 0)),
+            pl.BlockSpec((512, 1024), lambda h, t: (0, 0)),
+        ],
+        out_specs=pl.BlockSpec((1, 1, 512, 128 * WIDE), lambda h, t: (h, t, 0, 0)),
+        out_shape=shape(2, steps, 512, 128 * WIDE),
         compiler_params=params(),
         cost_estimate=cost(),
     )(after, rows, table)
@@ -330,59 +332,73 @@
     return jnp.concatenate([lr * gi + li * gr, li * gi - lr * gr], 0)
 
 
-def bubble_body(h, me_ref, g_ref, forward_ref, backward_ref, *refs):
-    held, (o_ref, rows_ref, result_ref, sems) = refs[:-4], refs[-4:]
+def bubble_body(h, me_ref, g_ref, forward_hbm, backward_hbm, *refs):
+    held, out_ref, scratch = refs[:-9], refs[-9], refs[-8:]
+    rows_ref, turned_ref, result_ref, o_ref, forward_ref, backward_ref, sems, others = scratch
     step = pl.program_id(0)
 
     @pl.when(step == 0)
     def _():
+        tables = [
+            pltpu.make_async_copy(forward_hbm, forward_ref, others.at[0]),
+            pltpu.make_async_copy(backward_hbm, backward_ref, others.at[1]),
+        ]
+        shards = [shard_at(me_ref[0], dz, dx, dc, -1) for dz, dx, dc in DISTANCES]
         copies = [
-            pltpu.make_async_copy(
-                arrived(held, h, dz, dx, dc),
-                rows_ref.at[shard_at(me_ref[0], dz, dx, dc, -1)],
-                sems.at[i],
-            )
-            for i, (dz, dx, dc) in enumerate(DISTANCES)
+            pltpu.make_async_copy(arrived(held, h, *way), rows_ref.at[i], sems.at[i])
+            for i, way in enumerate(DISTANCES)
         ]
-        for copy in copies:
+        for copy in copies + tables:
             copy.start()
+        for i, (copy, shard) in enumerate(zip(copies, shards)):
+            copy.wait()
+            tiles = rows_ref[i].reshape(4, 8, 8, 128)
+            row = pl.multiple_of(32 * shard, 32)
+            for t, tile in enumerate(swap_rows([tiles[:, j] for j in range(8)])):
+                turned_ref[t, pl.ds(row, 32), :] = tile.reshape(32, 128)
+        for copy in tables:
+            copy.wait()
+
+    x = jnp.concatenate([turned_ref[WIDE * step + i] for i in range(WIDE)], 1)
+    result = times(backward_ref, bubble(times(forward_ref, x), g_ref[0, 0]))
+    for i in range(WIDE):
+        result_ref[WIDE * step + i] = result[:, 128 * i : 128 * i + 128]
+
+    @pl.when(step == 8 // WIDE - 1)
+    def _():
+        copies = [pltpu.make_async_copy(o_ref.at[m], out_ref.at[m], sems.at[m]) for m in range(16)]
+        for m in range(16):
+            tiles = [
+                result_ref[t, 32 * m : 32 * m + 32, :].reshape(4, 8, 128) for t in range(8)
+            ]
+            o_ref[m] = jnp.stack(swap_rows(tiles), 1).reshape(256, 128)
+            copies[m].start()
         for copy in copies:
             copy.wait()
 
-    rows = rows_ref.reshape(4096, 128)
-    x = jnp.concatenate([rows[pl.ds(2 * step + i, 512, stride=8), :] for i in range(2)], 1)
-    result = times(backward_ref, bubble(times(forward_ref, x), g_ref[0, 0]))
-    for i in range(2):
-        result_ref[2 * step + i] = result[:, 128 * i : 128 * i + 128]
-
-    @pl.when(step == 3)
-    def _():
-        def shard(m, carry):
-            row = pl.multiple_of(32 * m, 32)
-            tiles = [result_ref[t, pl.ds(row, 32), :].reshape(4, 8, 128) for t in range(8)]
-            o_ref[m] = jnp.stack(swap_rows(tiles), 1).reshape(256, 128)
-            return carry
-
-        lax.fori_loop(0, 16, shard, 0)
-
-
-def bubble_transform(h, me, held, greater_disp, forward, backward):
-    table = pl.BlockSpec((512, 1024), lambda t: (0, 0))
+
+def bubble_transform(h, me, held, greater_disp, forward, backward, after=()):
     return pl.pallas_call(
         functools.partial(bubble_body, h),
-        grid=(4,),
-        in_specs=[SCALAR, pl.BlockSpec((1, 1, 512, 256), lambda t: (h, t, 0, 0)), table, table]
-        + [HBM] * len(held),
-        out_specs=pl.BlockSpec((16, 256, 128), lambda t: (0, 0, 0)),
+        grid=(8 // WIDE,),
+        in_specs=[SCALAR, pl.BlockSpec((1, 1, 512, 128 * WIDE), lambda t: (h, t, 0, 0)), HBM, HBM]
+        + [ANY] * len(held)
+        + [HBM] * len(after),
+        out_specs=HBM,
         out_shape=shape(16, 256, 128),
         scratch_shapes=[
             pltpu.VMEM((16, *BLOCK), F32),
             pltpu.VMEM((8, 512, 128), F32),
+            pltpu.VMEM((8, 512, 128), F32),
+            pltpu.VMEM((16, 256, 128), F32),
+            pltpu.VMEM((512, 1024), BF16),
+            pltpu.VMEM((512, 1024), BF16),
             pltpu.SemaphoreType.DMA((16,)),
-        ],
-        compiler_params=params(),
-        cost_estimate=cost(),
-    )(me, greater_disp, forward, backward, *held)
+            pltpu.SemaphoreType.DMA((2,)),
+        ],
+        compiler_params=params(),
+        cost_estimate=cost(),
+    )(me, greater_disp, forward, backward, *held, *after)
 
 
 def local(lesser, greater, site_of):
@@ -394,10 +410,10 @@
     ).reshape(16, 8, 8, 8, 128)
     sent = pack(me, greater_out, lesser.reshape(merged))
     forward, mirrored, backward = phase_tables(site_of)
-    near, far, disp = exchange(
+    near, far, crossing, disp = exchange(
         sent, (forward,), lambda turned: greater_transform(turned, greater_rows, mirrored)
     )
-    far = bubble_transform(1, me, far, disp, forward, backward)
+    far = bubble_transform(1, me, far, disp, forward, backward, (crossing,))
     far = lax.all_to_all(far, "mom", 0, 0, tiled=True).reshape(16, *BLOCK)
     near = bubble_transform(0, me, near, disp, forward, backward)
     near = lax.all_to_all(near, "mom", 0, 0, tiled=True).reshape(16, *BLOCK)

time: 207 us -> 203 us (0.981)
  Pallas kernels: 66.1 us -> 56 us
  waiting for transfers between devices: 93.9 us -> 99.8 us
    pallas_call x6, Pallas kernels: 43.6 us -> 33.5 us  [the longest x2 18 us: bubble_transform(): pl.pallas_call(functools.partial(bubble_body, h), grid=(8 // WIDE,), in_s...]
    all_to_all x1, waiting for transfers between devices: 10.9 us -> 14.9 us  [local(): far = lax.all_to_all(far, 'mom', 0, 0, tiled=True).reshape(16, *BLOCK)]
  transfers between devices with their start and end apart: 14 -> 14, of which waited for: 8 -> 7; matrix products, arithmetic and copies ran while one was open for 1% -> 1% of each run, Pallas kernels for 22% -> 20%
where the time goes in v4:
time: 203 us; the launch traced here: 199 us
  waiting for transfers between devices  99.8 us (49%)
  Pallas kernels  56 us (28%)
  starting transfers between devices  35.6 us (18%)
  local copies, waits for them, and re-layouts  7.5 us (4%)
    ppermute x11, waiting for transfers between devices, moved(): return lax.ppermute(values, 'mom', ways)  59.7 us
    all_to_all x1, waiting for transfers between devices, local(): near = lax.all_to_all(near, 'mom', 0, 0, tiled=True).reshape(16, *BLOCK)  25.2 us
    pallas_call x2, Pallas kernels, bubble_transform(): pl.pallas_call(functools.partial(bubble_body, h), grid=(8 // WIDE,), in_s...  18 us
    ppermute x11, starting transfers between devices, moved(): return lax.ppermute(values, 'mom', ways)  15.1 us
    all_to_all x1, waiting for transfers between devices, local(): far = lax.all_to_all(far, 'mom', 0, 0, tiled=True).reshape(16, *BLOCK)  14.9 us
    all_to_all x1, starting transfers between devices, local(): lax.all_to_all(greater_out.reshape(128, 64, 128), ('mom', 'tm'), 0, 0, ti...  10.7 us
    pallas_call x1, Pallas kernels, greater_transform(): pl.pallas_call(greater_body, grid=(2, steps), in_specs=[HBM, pl.BlockSpec...  8.66 us
    pallas_call x1, Pallas kernels, phase_tables(): pl.pallas_call(table_body, out_shape=(jax.ShapeDtypeStruct((512, 1024), B...  7.72 us
  transfers between devices with their start and end apart: 14, of which 7 were waited for; matrix products, arithmetic and copies ran while one was open for 1% of the time, Pallas kernels for 20%

profile of v4, /device:TPU:24, one launch (start us, length us, event | category | flops | bytes accessed | tf_op | source)
XLA Modules:
  0.0 199.3 jit_solution(10156968446999701350)
XLA Ops:
  0.0 5.4 %shard_map.37.after_ref = f32[4,4,8,8,8,128]{5,4,3,2,1,0:T(8,128)} custom-call(f32[2,16,4,32,256]{4,3,2,1,0:T(8,128)} %bitcast.12), custom_call_target="tpu_custom_call" | custom-call | flops 1 | bytes 1 | tf_op jit(solution)/shard_map/pallas_call | solution.py:270
  5.5 10.7 %all-to-all-start = ((f32[128,64,128]{2,1,0:T(8,128)}), f32[128,64,128]{2,1,0:T(8,128)}, u32[]{:S(2)}, u32[]{:S(2)}) async-start(f32[128,64,128]{2,1,0:T(8,128)} %bitcast.10), calls=%async_computation | async-start | bytes 8388608 | tf_op jit(solution)/shard_map/all_to_all | solution.py:408
  16.2 4.2 %shard_map.38 = (f32[4,2,2,16,8,128]{5,4,3,2,1,0:T(8,128)}, f32[4,2,2,16,8,128]{5,4,3,2,1,0:T(8,128)}, f32[2,2,2,16,8,128]{5,4,3,2,1,0:T(8,128)}, f32[2,2,2,16,8...) custom-call(s32[1]{0:T(128)} %bitcast.me_ref, ...), custom_call_target="tpu_custom_call" | custom-call | flops 1 | bytes 1 | tf_op jit(solution)/shard_map/pallas_call | solution.py:141
  20.4 1.8 collective-permute-start
  22.2 1.5 collective-permute-start.1
  23.7 2.7 %collective-permute-start.2 = (f32[2,2,2,16,8,128]{5,4,3,2,1,0:T(8,128)}, f32[2,2,2,16,8,128]{5,4,3,2,1,0:T(8,128)S(1)}, u32[]{:S(2)}, u32[]{:S(2)}) collective-permute-start(f32[2,2,2,16,8,128]{5,4,3,2,1,0:T(8,128)} %get-tuple-element.23), channel_id=1, source_target_pairs={{0,64},{8,72},{16,80},{24,88},{32,96},{40,104},{48,112},{56,120},{... | collective-permute-start | bytes 1572872 | tf_op jit(solution)/shard_map/ppermute | solution.py:120
  26.4 1.4 collective-permute-start.3
  28.7 0.9 reshape_reshape.8.result_ref
  30.5 7.7 %shard_map.39 = (bf16[512,1024]{1,0:T(8,128)(2,1)}, bf16[512,1024]{1,0:T(8,128)(2,1)}, bf16[512,1024]{1,0:T(8,128)(2,1)}) custom-call(s32[1,512]{1,0:T(1,128)} %reshape_reshape.6.lesser_ref, s32[1,512]{1,0:T(1,128)} %reshape.35.greater_ref, s32[512,1]{1,0:T(8,128)} %reshape_reshape.8.result_ref), custom_call_target="tpu_custom_call" | custom-call | flops 1 | bytes 1 | tf_op jit(solution)/shard_map/pallas_call | solution.py:69
  38.2 36.9 %collective-permute-done.1.refs_3_.refs_1_ = f32[2,2,2,16,8,128]{5,4,3,2,1,0:T(8,128)S(1)} collective-permute-done((f32[2,2,2,16,8,128]{5,4,3,2,1,0:T(8,128)}, f32[2,2,2,16,8,128]{5,4,3,2,1,0:T(8,128)S(1)}, u32[]{:S(2)}, u32[]{:S(2)}) %collective-permute-start.1) | collective-permute-done | bytes 524320 | tf_op jit(solution)/shard_map/ppermute | solution.py:120
  75.2 11.3 %collective-permute-done.2.refs_4_.refs_2_ = f32[2,2,2,16,8,128]{5,4,3,2,1,0:T(8,128)S(1)} collective-permute-done((f32[2,2,2,16,8,128]{5,4,3,2,1,0:T(8,128)}, f32[2,2,2,16,8,128]{5,4,3,2,1,0:T(8,128)S(1)}, u32[]{:S(2)}, u32[]{:S(2)}) %collective-permute-start.2) | collective-permute-done | bytes 524320 | tf_op jit(solution)/shard_map/ppermute | solution.py:120
  86.5 0.8 copy-done.3
  87.9 2.9 %shard_map.40 = (f32[4,2,16,8,128]{4,3,2,1,0:T(8,128)}, f32[4,2,16,8,128]{4,3,2,1,0:T(8,128)}, f32[4,2,16,8,128]{4,3,2,1,0:T(8,128)}, f32[4,2,16,8,128]{4,3,2,1,0:T(8,128)}, f32[4,2,16,8,128]{4,3,2,1,0:T(8,128)}) custom-call(f32[4,2,2,16,8,128]{5,4,3,2,1,0:T(8,128)} %get-tuple-element.19.refs_0_, f32[4,2,2,16,8,128]{5,4,3,2,1,0:T(8,128)} %copy-done, ...), custom_call_target="tpu_custom_call" | custom-call | flops 1 | bytes 1 | tf_op jit(solution)/shard_map/pallas_call | solution.py:169
  91.5 2.4 %collective-permute-start.5 = (f32[4,2,16,8,128]{4,3,2,1,0:T(8,128)}, f32[4,2,16,8,128]{4,3,2,1,0:T(8,128)S(1)}, u32[]{:S(2)}, u32[]{:S(2)}) collective-permute-start(f32[4,2,16,8,128]{4,3,2,1,0:T(8,128)} %get-tuple-element.30), channel_id=1, source_target_pairs={{0,64},{8,72},{16,80},{24,88},{32,96},{40,104},{48,112},{56,120},{... | collective-permute-start | bytes 1572872 | tf_op jit(solution)/shard_map/ppermute | solution.py:120
  93.9 1.9 collective-permute-start.6
  96.3 8.7 %shard_map.41.refs_5_.g_ref.refs_4_ = f32[2,2,512,512]{3,2,1,0:T(8,128)} custom-call(f32[4,2,16,8,128]{4,3,2,1,0:T(8,128)} %get-tuple-element.26.after_ref, f32[16,8,8,8,128]{4,3,2,1,0:T(8,128)} %bitcast.5.x_ref, bf16[512,1024]{1,0:T(8,128)(2,1)} %get-tuple-element.27.table_ref), custom_call_target="tpu_custom_call" | custom-call | flops 1 | bytes 1 | tf_op jit(solution)/shard_map/pallas_call | solution.py:314
  105.0 1.8 shard_map.44
  106.8 1.6 collective-permute-start.10
  108.5 8.8 %collective-permute-done.5.refs_3_ = f32[4,2,16,8,128]{4,3,2,1,0:T(8,128)S(1)} collective-permute-done((f32[4,2,16,8,128]{4,3,2,1,0:T(8,128)}, f32[4,2,16,8,128]{4,3,2,1,0:T(8,128)S(1)}, u32[]{:S(2)}, u32[]{:S(2)}) %collective-permute-start.5) | collective-permute-done | bytes 524320 | tf_op jit(solution)/shard_map/ppermute | solution.py:120
  118.1 0.8 copy-done.8
  118.9 2.1 %shard_map.42.refs_7_ = f32[8,2,16,8,128]{4,3,2,1,0:T(8,128)} custom-call(f32[4,2,2,16,8,128]{5,4,3,2,1,0:T(8,128)} %get-tuple-element.19.refs_0_, f32[4,2,2,16,8,128]{5,4,3,2,1,0:T(8,128)} %copy-done, f32[4,2,16,8,128]{4,3,2,1,0:T(8,128)} %copy-done.6, f32[4,2,16,8,128]{4,3,2,1,0:T(8,128)} %copy-done.7, f32[4,2,16,8,128]{4,3,2,1,0:T(8,128)} %copy-done.8, ...), custom_call_target="tpu_custom_call" | custom-call | flops 1 | bytes 1 | tf_op jit(solution)/shard_map/pallas_call | solution.py:169
  121.1 0.7 copy-done.11
  122.2 9.0 %shard_map.45 = f32[16,256,128]{2,1,0:T(8,128)} custom-call(s32[1]{0:T(128)} %bitcast.me_ref, f32[2,2,512,512]{3,2,1,0:T(8,128)} %shard_map.41.refs_5_.g_ref.refs_4_, bf16[512,1024]{1,0:T(8,128)(2,1)} %get-tuple-element.25.refs_6_.forward_hbm, bf16[512,1024]{1,0:T(8,128)(2,1)} %get-tuple-element.28.backward_hbm, ...), custom_call_target="tpu_custom_call" | custom-call | flops 1 | bytes 1 | tf_op jit(solution)/shard_map/pallas_call | solution.py:381
  131.3 4.9 %all-to-all-start.2 = ((f32[16,256,128]{2,1,0:T(8,128)}), f32[16,256,128]{2,1,0:T(8,128)S(1)}, u32[]{:S(2)}, u32[]{:S(2)}) async-start(f32[16,256,128]{2,1,0:T(8,128)} %shard_map.45), calls=%async_computation.2 | async-start | bytes 4194304 | tf_op jit(solution)/shard_map/all_to_all | solution.py:417
  136.6 2.3 %collective-permute-done.7.refs_5_ = f32[8,2,16,8,128]{4,3,2,1,0:T(8,128)S(1)} collective-permute-done((f32[8,2,16,8,128]{4,3,2,1,0:T(8,128)S(1)}, f32[8,2,16,8,128]{4,3,2,1,0:T(8,128)S(1)}, u32[]{:S(2)}, u32[]{:S(2)}) %collective-permute-start.7) | collective-permute-done | bytes 1048608 | tf_op jit(solution)/shard_map/ppermute | solution.py:120
  138.9 1.0 copy-done.9
  140.0 9.0 %shard_map.43 = f32[16,256,128]{2,1,0:T(8,128)} custom-call(s32[1]{0:T(128)} %bitcast.me_ref, f32[2,2,512,512]{3,2,1,0:T(8,128)} %shard_map.41.refs_5_.g_ref.refs_4_, bf16[512,1024]{1,0:T(8,128)(2,1)} %get-tuple-element.25.refs_6_.forward_hbm, bf16[512,1024]{1,0:T(8,128)(2,1)} %get-tuple-element.28.backward_hbm, ...), custom_call_target="tpu_custom_call" | custom-call | flops 1 | bytes 1 | tf_op jit(solution)/shard_map/pallas_call | solution.py:381
  149.0 14.9 %all-to-all-done.2 = f32[16,256,128]{2,1,0:T(8,128)S(1)} async-done(((f32[16,256,128]{2,1,0:T(8,128)}), f32[16,256,128]{2,1,0:T(8,128)S(1)}, u32[]{:S(2)}, u32[]{:S(2)}) %all-to-all-start.2) | async-done | bytes 2097184 | tf_op jit(solution)/shard_map/all_to_all | solution.py:417
  163.9 4.9 %all-to-all-start.1 = ((f32[16,256,128]{2,1,0:T(8,128)}), f32[16,256,128]{2,1,0:T(8,128)}, u32[]{:S(2)}, u32[]{:S(2)}) async-start(f32[16,256,128]{2,1,0:T(8,128)} %shard_map.43), calls=%async_computation.1 | async-start | bytes 4194304 | tf_op jit(solution)/shard_map/all_to_all | solution.py:419
  168.8 2.6 %shard_map.46.refs_1_ = f32[2,16,4,32,256]{4,3,2,1,0:T(8,128)} custom-call(f32[16,2,16,8,128]{4,3,2,1,0:T(8,128)} %bitcast.11), custom_call_target="tpu_custom_call" | custom-call | flops 1 | bytes 1 | tf_op jit(solution)/shard_map/pallas_call | solution.py:227
  171.4 25.2 %all-to-all-done.1 = f32[16,256,128]{2,1,0:T(8,128)} async-done(((f32[16,256,128]{2,1,0:T(8,128)}), f32[16,256,128]{2,1,0:T(8,128)}, u32[]{:S(2)}, u32[]{:S(2)}) %all-to-all-start.1) | async-done | bytes 2097184 | tf_op jit(solution)/shard_map/all_to_all | solution.py:419
  196.6 2.6 %shard_map.47 = f32[2,16,4,32,256]{4,3,2,1,0:T(8,128)} custom-call(f32[16,2,16,8,128]{4,3,2,1,0:T(8,128)} %bitcast.6.refs_0_, f32[2,16,4,32,256]{4,3,2,1,0:T(8,128)} %shard_map.46.refs_1_), custom_call_target="tpu_custom_call", output_to_operand_aliasing={{}: (1, {})} | custom-call | flops 1 | bytes 1 | tf_op jit(solution)/shard_map/pallas_call | solution.py:227
  (45 shorter events, 5.4 us)
Async XLA Ops:
  5.5 90.9 %all-to-all-start = ((f32[128,64,128]{2,1,0:T(8,128)}), f32[128,64,128]{2,1,0:T(8,128)}, u32[]{:S(2)}, u32[]{:S(2)}) async-start(f32[128,64,128]{2,1,0:T(8,128)} %bitcast.10), calls=%async_computation | async-start | bytes 8388608 | tf_op jit(solution)/shard_map/all_to_all | solution.py:408
  16.2 11.6 %copy-start.13 = (s32[256]{0:T(256)S(1)}, s32[256]{0:T(256)}, u32[]{:S(2)}) copy-start(s32[256]{0:T(256)} %param.5) | copy-start | bytes 3076
  20.4 66.1 %collective-permute-start = (f32[4,2,2,16,8,128]{5,4,3,2,1,0:T(8,128)}, f32[4,2,2,16,8,128]{5,4,3,2,1,0:T(8,128)S(1)}, u32[]{:S(2)}, u32[]{:S(2)}) collective-permute-start(f32[4,2,2,16,8,128]{5,4,3,2,1,0:T(8,128)} %get-tuple-element.20), channel_id=1, source_target_pairs={{0,16},{8,24},{16,0},{24,8},{32,48},{40,56},{48,32},{56,40},{64,80... | collective-permute-start | bytes 3145736 | tf_op jit(solution)/shard_map/ppermute | solution.py:120
  22.2 53.0 %collective-permute-start.1 = (f32[2,2,2,16,8,128]{5,4,3,2,1,0:T(8,128)}, f32[2,2,2,16,8,128]{5,4,3,2,1,0:T(8,128)S(1)}, u32[]{:S(2)}, u32[]{:S(2)}) collective-permute-start(f32[2,2,2,16,8,128]{5,4,3,2,1,0:T(8,128)} %get-tuple-element.22), channel_id=1, source_target_pairs={{0,32},{8,40},{16,48},{24,56},{32,64},{40,72},{48,80},{56,88},{64,... | collective-permute-start | bytes 1572872 | tf_op jit(solution)/shard_map/ppermute | solution.py:120
  23.7 62.8 %collective-permute-start.2 = (f32[2,2,2,16,8,128]{5,4,3,2,1,0:T(8,128)}, f32[2,2,2,16,8,128]{5,4,3,2,1,0:T(8,128)S(1)}, u32[]{:S(2)}, u32[]{:S(2)}) collective-permute-start(f32[2,2,2,16,8,128]{5,4,3,2,1,0:T(8,128)} %get-tuple-element.23), channel_id=1, source_target_pairs={{0,64},{8,72},{16,80},{24,88},{32,96},{40,104},{48,112},{56,120},{... | collective-permute-start | bytes 1572872 | tf_op jit(solution)/shard_map/ppermute | solution.py:120
  26.4 60.1 %collective-permute-start.3 = (f32[2,2,2,16,8,128]{5,4,3,2,1,0:T(8,128)}, f32[2,2,2,16,8,128]{5,4,3,2,1,0:T(8,128)S(1)}, u32[]{:S(2)}, u32[]{:S(2)}) collective-permute-start(f32[2,2,2,16,8,128]{5,4,3,2,1,0:T(8,128)} %get-tuple-element.24), channel_id=1, source_target_pairs={{0,96},{8,104},{16,112},{24,120},{32,0},{40,8},{48,16},{56,24},{64... | collective-permute-start | bytes 1572872 | tf_op jit(solution)/shard_map/ppermute | solution.py:120
  75.2 11.3 %copy-start.2 = (f32[2,2,2,16,8,128]{5,4,3,2,1,0:T(8,128)}, f32[2,2,2,16,8,128]{5,4,3,2,1,0:T(8,128)S(1)}, u32[]{:S(2)}) copy-start(f32[2,2,2,16,8,128]{5,4,3,2,1,0:T(8,128)S(1)} %collective-permute-done.1.refs_3_.refs_1_) | copy-start | bytes 1572868
  86.5 0.8 copy-start.3
  86.5 1.0 copy-start.4
  86.5 1.4 copy-start
  90.8 16.0 %collective-permute-start.4 = (f32[4,2,16,8,128]{4,3,2,1,0:T(8,128)}, f32[4,2,16,8,128]{4,3,2,1,0:T(8,128)S(1)}, u32[]{:S(2)}, u32[]{:S(2)}) collective-permute-start(f32[4,2,16,8,128]{4,3,2,1,0:T(8,128)} %get-tuple-element.29), channel_id=1, source_target_pairs={{0,32},{8,40},{16,48},{24,56},{32,64},{40,72},{48,80},{56,88},{64,... | collective-permute-start | bytes 1572872 | tf_op jit(solution)/shard_map/ppermute | solution.py:120
  91.5 25.7 %collective-permute-start.5 = (f32[4,2,16,8,128]{4,3,2,1,0:T(8,128)}, f32[4,2,16,8,128]{4,3,2,1,0:T(8,128)S(1)}, u32[]{:S(2)}, u32[]{:S(2)}) collective-permute-start(f32[4,2,16,8,128]{4,3,2,1,0:T(8,128)} %get-tuple-element.30), channel_id=1, source_target_pairs={{0,64},{8,72},{16,80},{24,88},{32,96},{40,104},{48,112},{56,120},{... | collective-permute-start | bytes 1572872 | tf_op jit(solution)/shard_map/ppermute | solution.py:120
  93.9 23.7 %collective-permute-start.6 = (f32[4,2,16,8,128]{4,3,2,1,0:T(8,128)}, f32[4,2,16,8,128]{4,3,2,1,0:T(8,128)S(1)}, u32[]{:S(2)}, u32[]{:S(2)}) collective-permute-start(f32[4,2,16,8,128]{4,3,2,1,0:T(8,128)} %get-tuple-element.31), channel_id=1, source_target_pairs={{0,96},{8,104},{16,112},{24,120},{32,0},{40,8},{48,16},{56,24},{64... | collective-permute-start | bytes 1572872 | tf_op jit(solution)/shard_map/ppermute | solution.py:120
  95.7 25.3 %collective-permute-start.8 = (f32[4,2,16,8,128]{4,3,2,1,0:T(8,128)}, f32[4,2,16,8,128]{4,3,2,1,0:T(8,128)S(1)}, u32[]{:S(2)}, u32[]{:S(2)}) collective-permute-start(f32[4,2,16,8,128]{4,3,2,1,0:T(8,128)} %get-tuple-element.26.after_ref), channel_id=1, source_target_pairs={{0,16},{8,24},{16,0},{24,8},{32,48},{40,56},{48,32},{56,40},{64,80... | collective-permute-start | bytes 1572872 | tf_op jit(solution)/shard_map/ppermute | solution.py:120
  96.3 8.7 %copy-start.14 = (f32[4,2,16,8,128]{4,3,2,1,0:T(8,128)S(1)}, f32[4,2,16,8,128]{4,3,2,1,0:T(8,128)}, u32[]{:S(2)}) copy-start(f32[4,2,16,8,128]{4,3,2,1,0:T(8,128)} %get-tuple-element.32) | copy-start | bytes 1572868
  105.0 16.0 %collective-permute-start.9 = (f32[4,2,16,8,128]{4,3,2,1,0:T(8,128)S(1)}, f32[4,2,16,8,128]{4,3,2,1,0:T(8,128)S(1)}, u32[]{:S(2)}, u32[]{:S(2)}) collective-permute-start(f32[4,2,16,8,128]{4,3,2,1,0:T(8,128)S(1)} %copy-done.14), channel_id=1, source_target_pairs={{0,24},{8,16},{16,8},{24,0},{32,56},{40,48},{48,40},{56,32},{64,88... | collective-permute-start | bytes 1572872 | tf_op jit(solution)/shard_map/ppermute | solution.py:120
  106.8 10.8 %copy-start.6 = (f32[4,2,16,8,128]{4,3,2,1,0:T(8,128)}, f32[4,2,16,8,128]{4,3,2,1,0:T(8,128)S(1)}, u32[]{:S(2)}) copy-start(f32[4,2,16,8,128]{4,3,2,1,0:T(8,128)S(1)} %collective-permute-done.4.refs_2_) | copy-start | bytes 1572868
  106.8 14.2 %collective-permute-start.10 = (f32[4,2,16,8,128]{4,3,2,1,0:T(8,128)}, f32[4,2,16,8,128]{4,3,2,1,0:T(8,128)S(1)}, u32[]{:S(2)}, u32[]{:S(2)}) collective-permute-start(f32[4,2,16,8,128]{4,3,2,1,0:T(8,128)} %shard_map.44), channel_id=1, source_target_pairs={{0,8},{8,0},{16,24},{24,16},{32,40},{40,32},{48,56},{56,48},{64,72... | collective-permute-start | bytes 1572872 | tf_op jit(solution)/shard_map/ppermute | solution.py:120
  117.2 0.8 copy-start.7
  118.0 0.8 copy-start.8
  121.0 0.8 copy-start.11
  121.0 1.0 copy-start.10
  121.0 1.2 copy-start.12
  131.2 4.9 %copy-start.5 = (f32[8,2,16,8,128]{4,3,2,1,0:T(8,128)S(1)}, f32[8,2,16,8,128]{4,3,2,1,0:T(8,128)}, u32[]{:S(2)}) copy-start(f32[8,2,16,8,128]{4,3,2,1,0:T(8,128)} %shard_map.42.refs_7_) | copy-start | bytes 3145732
  131.3 32.6 %all-to-all-start.2 = ((f32[16,256,128]{2,1,0:T(8,128)}), f32[16,256,128]{2,1,0:T(8,128)S(1)}, u32[]{:S(2)}, u32[]{:S(2)}) async-start(f32[16,256,128]{2,1,0:T(8,128)} %shard_map.45), calls=%async_computation.2 | async-start | bytes 4194304 | tf_op jit(solution)/shard_map/all_to_all | solution.py:417
  136.2 2.8 %collective-permute-start.7 = (f32[8,2,16,8,128]{4,3,2,1,0:T(8,128)S(1)}, f32[8,2,16,8,128]{4,3,2,1,0:T(8,128)S(1)}, u32[]{:S(2)}, u32[]{:S(2)}) collective-permute-start(f32[8,2,16,8,128]{4,3,2,1,0:T(8,128)S(1)} %copy-done.5), channel_id=1, source_target_pairs={{0,8},{8,0},{16,24},{24,16},{32,40},{40,32},{48,56},{56,48},{64,72... | collective-permute-start | bytes 3145736 | tf_op jit(solution)/shard_map/ppermute | solution.py:120
  138.9 1.0 copy-start.9
  163.9 4.9 %copy-start.1 = (f32[16,256,128]{2,1,0:T(8,128)}, f32[16,256,128]{2,1,0:T(8,128)S(1)}, u32[]{:S(2)}) copy-start(f32[16,256,128]{2,1,0:T(8,128)S(1)} %all-to-all-done.2) | copy-start | bytes 6291460
  163.9 32.7 %all-to-all-start.1 = ((f32[16,256,128]{2,1,0:T(8,128)}), f32[16,256,128]{2,1,0:T(8,128)}, u32[]{:S(2)}, u32[]{:S(2)}) async-start(f32[16,256,128]{2,1,0:T(8,128)} %shard_map.43), calls=%async_computation.1 | async-start | bytes 4194304 | tf_op jit(solution)/shard_map/all_to_all | solution.py:419

commit v5 on v4

--- a/solution.py
+++ b/solution.py
@@ -9,7 +9,7 @@
 from jax.sharding import PartitionSpec as P
 
 L = 16
-VMEM = 56 * 1024 * 1024
+VMEM = 63 * 1024 * 1024
 F32 = jnp.float32
 BF16 = jnp.bfloat16
 BLOCK = (2, 16, 8, 128)

time: 203 us -> 200 us (0.985)
  local copies, waits for them, and re-layouts: 7.5 us -> 2.74 us
    unnamed x30 -> x8, local copies, waits for them, and re-layouts: 4.86 us -> 0.02 us
where the time goes in v5:
time: 200 us; the launch traced here: 196 us
  waiting for transfers between devices  101 us (50%)
  Pallas kernels  55.9 us (28%)
  starting transfers between devices  36.3 us (18%)
  local copies, waits for them, and re-layouts  2.74 us (1%)
    ppermute x11, waiting for transfers between devices, moved(): return lax.ppermute(values, 'mom', ways)  59.7 us
    all_to_all x1, waiting for transfers between devices, local(): near = lax.all_to_all(near, 'mom', 0, 0, tiled=True).reshape(16, *BLOCK)  25.2 us
    pallas_call x2, Pallas kernels, bubble_transform(): pl.pallas_call(functools.partial(bubble_body, h), grid=(8 // WIDE,), in_s...  18 us
    all_to_all x1, waiting for transfers between devices, local(): far = lax.all_to_all(far, 'mom', 0, 0, tiled=True).reshape(16, *BLOCK)  15.9 us
    ppermute x11, starting transfers between devices, moved(): return lax.ppermute(values, 'mom', ways)  15.3 us
    all_to_all x1, starting transfers between devices, local(): lax.all_to_all(greater_out.reshape(128, 64, 128), ('mom', 'tm'), 0, 0, ti...  10.7 us
    pallas_call x1, Pallas kernels, greater_transform(): pl.pallas_call(greater_body, grid=(2, steps), in_specs=[HBM, pl.BlockSpec...  8.59 us
    pallas_call x1, Pallas kernels, phase_tables(): pl.pallas_call(table_body, out_shape=(jax.ShapeDtypeStruct((512, 1024), B...  7.75 us
  transfers between devices with their start and end apart: 14, of which 7 were waited for; matrix products, arithmetic and copies ran while one was open for 1% of the time, Pallas kernels for 20%

profile of v5, /device:TPU:24, one launch (start us, length us, event | category | flops | bytes accessed | tf_op | source)
XLA Modules:
  0.0 196.2 jit_solution(5699706656102297427)
XLA Ops:
  0.0 5.4 %shard_map.37.after_ref = f32[4,4,8,8,8,128]{5,4,3,2,1,0:T(8,128)} custom-call(f32[2,16,4,32,256]{4,3,2,1,0:T(8,128)} %bitcast.11), custom_call_target="tpu_custom_call" | custom-call | flops 1 | bytes 1 | tf_op jit(solution)/shard_map/pallas_call | solution.py:270
  5.5 10.7 %all-to-all-start = ((f32[128,64,128]{2,1,0:T(8,128)}), f32[128,64,128]{2,1,0:T(8,128)}, u32[]{:S(2)}, u32[]{:S(2)}) async-start(f32[128,64,128]{2,1,0:T(8,128)} %bitcast.10), calls=%async_computation | async-start | bytes 8388608 | tf_op jit(solution)/shard_map/all_to_all | solution.py:408
  16.2 4.2 %shard_map.38 = (f32[4,2,2,16,8,128]{5,4,3,2,1,0:T(8,128)}, f32[4,2,2,16,8,128]{5,4,3,2,1,0:T(8,128)}, f32[2,2,2,16,8,128]{5,4,3,2,1,0:T(8,128)}, f32[2,2,2,16,8...) custom-call(s32[1]{0:T(128)} %bitcast.me_ref, ...), custom_call_target="tpu_custom_call" | custom-call | flops 1 | bytes 1 | tf_op jit(solution)/shard_map/pallas_call | solution.py:141
  20.4 1.8 collective-permute-start
  22.2 1.5 collective-permute-start.1
  23.7 2.7 %collective-permute-start.2 = (f32[2,2,2,16,8,128]{5,4,3,2,1,0:T(8,128)}, f32[2,2,2,16,8,128]{5,4,3,2,1,0:T(8,128)}, u32[]{:S(2)}, u32[]{:S(2)}) collective-permute-start(f32[2,2,2,16,8,128]{5,4,3,2,1,0:T(8,128)} %get-tuple-element.23), channel_id=1, source_target_pairs={{0,64},{8,72},{16,80},{24,88},{32,96},{40,104},{48,112},{56,120},{... | collective-permute-start | bytes 1572872 | tf_op jit(solution)/shard_map/ppermute | solution.py:120
  26.4 1.4 collective-permute-start.3
  28.0 0.7 reshape_reshape.6.lesser_ref
  28.7 0.9 reshape_reshape.8.result_ref
  29.8 0.7 reshape.35.greater_ref
  30.6 7.7 %shard_map.39 = (bf16[512,1024]{1,0:T(8,128)(2,1)}, bf16[512,1024]{1,0:T(8,128)(2,1)}, bf16[512,1024]{1,0:T(8,128)(2,1)}) custom-call(s32[1,512]{1,0:T(1,128)} %reshape_reshape.6.lesser_ref, s32[1,512]{1,0:T(1,128)} %reshape.35.greater_ref, s32[512,1]{1,0:T(8,128)} %reshape_reshape.8.result_ref), custom_call_target="tpu_custom_call" | custom-call | flops 1 | bytes 1 | tf_op jit(solution)/shard_map/pallas_call | solution.py:69
  38.3 36.9 %collective-permute-done.1.refs_3_.refs_1_ = f32[2,2,2,16,8,128]{5,4,3,2,1,0:T(8,128)S(1)} collective-permute-done((f32[2,2,2,16,8,128]{5,4,3,2,1,0:T(8,128)}, f32[2,2,2,16,8,128]{5,4,3,2,1,0:T(8,128)S(1)}, u32[]{:S(2)}, u32[]{:S(2)}) %collective-permute-start.1) | collective-permute-done | bytes 524320 | tf_op jit(solution)/shard_map/ppermute | solution.py:120
  75.2 11.4 %collective-permute-done.2.refs_4_.refs_2_ = f32[2,2,2,16,8,128]{5,4,3,2,1,0:T(8,128)} collective-permute-done((f32[2,2,2,16,8,128]{5,4,3,2,1,0:T(8,128)}, f32[2,2,2,16,8,128]{5,4,3,2,1,0:T(8,128)}, u32[]{:S(2)}, u32[]{:S(2)}) %collective-permute-start.2) | collective-permute-done | bytes 524320 | tf_op jit(solution)/shard_map/ppermute | solution.py:120
  86.6 2.8 %shard_map.40 = (f32[4,2,16,8,128]{4,3,2,1,0:T(8,128)}, f32[4,2,16,8,128]{4,3,2,1,0:T(8,128)}, f32[4,2,16,8,128]{4,3,2,1,0:T(8,128)}, f32[4,2,16,8,128]{4,3,2,1,0:T(8,128)}, f32[4,2,16,8,128]{4,3,2,1,0:T(8,128)}) custom-call(f32[4,2,2,16,8,128]{5,4,3,2,1,0:T(8,128)} %get-tuple-element.19.refs_0_, f32[4,2,2,16,8,128]{5,4,3,2,1,0:T(8,128)} %collective-permute-done.refs_1_, ...), custom_call_target="tpu_custom_call" | custom-call | flops 1 | bytes 1 | tf_op jit(solution)/shard_map/pallas_call | solution.py:169
  89.4 1.0 collective-permute-start.4
  90.4 2.4 %collective-permute-start.5 = (f32[4,2,16,8,128]{4,3,2,1,0:T(8,128)}, f32[4,2,16,8,128]{4,3,2,1,0:T(8,128)}, u32[]{:S(2)}, u32[]{:S(2)}) collective-permute-start(f32[4,2,16,8,128]{4,3,2,1,0:T(8,128)} %get-tuple-element.30), channel_id=1, source_target_pairs={{0,64},{8,72},{16,80},{24,88},{32,96},{40,104},{48,112},{56,120},{... | collective-permute-start | bytes 1572872 | tf_op jit(solution)/shard_map/ppermute | solution.py:120
  92.8 1.9 collective-permute-start.6
  94.7 0.6 collective-permute-start.8
  95.2 8.6 %shard_map.41.refs_5_.g_ref.refs_4_ = f32[2,2,512,512]{3,2,1,0:T(8,128)} custom-call(f32[4,2,16,8,128]{4,3,2,1,0:T(8,128)} %get-tuple-element.26.after_ref, f32[16,8,8,8,128]{4,3,2,1,0:T(8,128)} %bitcast.5.x_ref, bf16[512,1024]{1,0:T(8,128)(2,1)} %get-tuple-element.27.table_ref), custom_call_target="tpu_custom_call" | custom-call | flops 1 | bytes 1 | tf_op jit(solution)/shard_map/pallas_call | solution.py:314
  103.8 1.8 shard_map.44
  105.7 1.6 collective-permute-start.10
  107.3 8.9 %collective-permute-done.5.refs_3_ = f32[4,2,16,8,128]{4,3,2,1,0:T(8,128)} collective-permute-done((f32[4,2,16,8,128]{4,3,2,1,0:T(8,128)}, f32[4,2,16,8,128]{4,3,2,1,0:T(8,128)}, u32[]{:S(2)}, u32[]{:S(2)}) %collective-permute-start.5) | collective-permute-done | bytes 524320 | tf_op jit(solution)/shard_map/ppermute | solution.py:120
  116.3 2.1 %shard_map.42.refs_7_ = f32[8,2,16,8,128]{4,3,2,1,0:T(8,128)} custom-call(f32[4,2,2,16,8,128]{5,4,3,2,1,0:T(8,128)} %get-tuple-element.19.refs_0_, f32[4,2,2,16,8,128]{5,4,3,2,1,0:T(8,128)} %collective-permute-done.refs_1_, f32[4,2,16,8,128]{4,3,2,1,0:T(8,128)} %copy-done.2, f32[4,2,16,8,128]{4,3,2,1,0:T(8,128)} %collective-permute-done.5.refs_3_, ...), custom_call_target="tpu_custom_call" | custom-call | flops 1 | bytes 1 | tf_op jit(solution)/shard_map/pallas_call | solution.py:169
  118.5 9.1 %shard_map.45 = f32[16,256,128]{2,1,0:T(8,128)} custom-call(s32[1]{0:T(128)} %bitcast.me_ref, f32[2,2,512,512]{3,2,1,0:T(8,128)} %shard_map.41.refs_5_.g_ref.refs_4_, bf16[512,1024]{1,0:T(8,128)(2,1)} %get-tuple-element.25.refs_6_.forward_hbm, bf16[512,1024]{1,0:T(8,128)(2,1)} %get-tuple-element.28.backward_hbm, ...), custom_call_target="tpu_custom_call" | custom-call | flops 1 | bytes 1 | tf_op jit(solution)/shard_map/pallas_call | solution.py:381
  127.6 5.4 %all-to-all-start.2 = ((f32[16,256,128]{2,1,0:T(8,128)}), f32[16,256,128]{2,1,0:T(8,128)}, u32[]{:S(2)}, u32[]{:S(2)}) async-start(f32[16,256,128]{2,1,0:T(8,128)} %shard_map.45), calls=%async_computation.2 | async-start | bytes 4194304 | tf_op jit(solution)/shard_map/all_to_all | solution.py:417
  133.4 2.4 %collective-permute-done.7.refs_5_ = f32[8,2,16,8,128]{4,3,2,1,0:T(8,128)} collective-permute-done((f32[8,2,16,8,128]{4,3,2,1,0:T(8,128)S(1)}, f32[8,2,16,8,128]{4,3,2,1,0:T(8,128)}, u32[]{:S(2)}, u32[]{:S(2)}) %collective-permute-start.7) | collective-permute-done | bytes 1048608 | tf_op jit(solution)/shard_map/ppermute | solution.py:120
  135.8 9.0 %shard_map.43 = f32[16,256,128]{2,1,0:T(8,128)} custom-call(s32[1]{0:T(128)} %bitcast.me_ref, f32[2,2,512,512]{3,2,1,0:T(8,128)} %shard_map.41.refs_5_.g_ref.refs_4_, bf16[512,1024]{1,0:T(8,128)(2,1)} %get-tuple-element.25.refs_6_.forward_hbm, bf16[512,1024]{1,0:T(8,128)(2,1)} %get-tuple-element.28.backward_hbm, ...), custom_call_target="tpu_custom_call" | custom-call | flops 1 | bytes 1 | tf_op jit(solution)/shard_map/pallas_call | solution.py:381
  144.8 15.9 %all-to-all-done.2 = f32[16,256,128]{2,1,0:T(8,128)} async-done(((f32[16,256,128]{2,1,0:T(8,128)}), f32[16,256,128]{2,1,0:T(8,128)}, u32[]{:S(2)}, u32[]{:S(2)}) %all-to-all-start.2) | async-done | bytes 2097184 | tf_op jit(solution)/shard_map/all_to_all | solution.py:417
  160.8 4.9 %all-to-all-start.1 = ((f32[16,256,128]{2,1,0:T(8,128)}), f32[16,256,128]{2,1,0:T(8,128)}, u32[]{:S(2)}, u32[]{:S(2)}) async-start(f32[16,256,128]{2,1,0:T(8,128)} %shard_map.43), calls=%async_computation.1 | async-start | bytes 4194304 | tf_op jit(solution)/shard_map/all_to_all | solution.py:419
  165.7 2.6 %shard_map.46.refs_1_ = f32[2,16,4,32,256]{4,3,2,1,0:T(8,128)} custom-call(f32[16,2,16,8,128]{4,3,2,1,0:T(8,128)} %bitcast.7.refs_0_), custom_call_target="tpu_custom_call" | custom-call | flops 1 | bytes 1 | tf_op jit(solution)/shard_map/pallas_call | solution.py:227
  168.2 25.2 %all-to-all-done.1 = f32[16,256,128]{2,1,0:T(8,128)} async-done(((f32[16,256,128]{2,1,0:T(8,128)}), f32[16,256,128]{2,1,0:T(8,128)}, u32[]{:S(2)}, u32[]{:S(2)}) %all-to-all-start.1) | async-done | bytes 2097184 | tf_op jit(solution)/shard_map/all_to_all | solution.py:419
  193.4 2.6 %shard_map.47 = f32[2,16,4,32,256]{4,3,2,1,0:T(8,128)} custom-call(f32[16,2,16,8,128]{4,3,2,1,0:T(8,128)} %bitcast.6.refs_0_, f32[2,16,4,32,256]{4,3,2,1,0:T(8,128)} %shard_map.46.refs_1_), custom_call_target="tpu_custom_call", output_to_operand_aliasing={{}: (1, {})} | custom-call | flops 1 | bytes 1 | tf_op jit(solution)/shard_map/pallas_call | solution.py:227
  (23 shorter events, 1.0 us)
Async XLA Ops:
  5.5 89.8 %all-to-all-start = ((f32[128,64,128]{2,1,0:T(8,128)}), f32[128,64,128]{2,1,0:T(8,128)}, u32[]{:S(2)}, u32[]{:S(2)}) async-start(f32[128,64,128]{2,1,0:T(8,128)} %bitcast.10), calls=%async_computation | async-start | bytes 8388608 | tf_op jit(solution)/shard_map/all_to_all | solution.py:408
  16.2 11.6 %copy-start.3 = (s32[256]{0:T(256)S(1)}, s32[256]{0:T(256)}, u32[]{:S(2)}) copy-start(s32[256]{0:T(256)} %param.5) | copy-start | bytes 3076
  20.4 66.2 %collective-permute-start = (f32[4,2,2,16,8,128]{5,4,3,2,1,0:T(8,128)}, f32[4,2,2,16,8,128]{5,4,3,2,1,0:T(8,128)}, u32[]{:S(2)}, u32[]{:S(2)}) collective-permute-start(f32[4,2,2,16,8,128]{5,4,3,2,1,0:T(8,128)} %get-tuple-element.20), channel_id=1, source_target_pairs={{0,16},{8,24},{16,0},{24,8},{32,48},{40,56},{48,32},{56,40},{64,80... | collective-permute-start | bytes 3145736 | tf_op jit(solution)/shard_map/ppermute | solution.py:120
  22.2 53.0 %collective-permute-start.1 = (f32[2,2,2,16,8,128]{5,4,3,2,1,0:T(8,128)}, f32[2,2,2,16,8,128]{5,4,3,2,1,0:T(8,128)S(1)}, u32[]{:S(2)}, u32[]{:S(2)}) collective-permute-start(f32[2,2,2,16,8,128]{5,4,3,2,1,0:T(8,128)} %get-tuple-element.22), channel_id=1, source_target_pairs={{0,32},{8,40},{16,48},{24,56},{32,64},{40,72},{48,80},{56,88},{64,... | collective-permute-start | bytes 1572872 | tf_op jit(solution)/shard_map/ppermute | solution.py:120
  23.7 62.9 %collective-permute-start.2 = (f32[2,2,2,16,8,128]{5,4,3,2,1,0:T(8,128)}, f32[2,2,2,16,8,128]{5,4,3,2,1,0:T(8,128)}, u32[]{:S(2)}, u32[]{:S(2)}) collective-permute-start(f32[2,2,2,16,8,128]{5,4,3,2,1,0:T(8,128)} %get-tuple-element.23), channel_id=1, source_target_pairs={{0,64},{8,72},{16,80},{24,88},{32,96},{40,104},{48,112},{56,120},{... | collective-permute-start | bytes 1572872 | tf_op jit(solution)/shard_map/ppermute | solution.py:120
  26.4 60.2 %collective-permute-start.3 = (f32[2,2,2,16,8,128]{5,4,3,2,1,0:T(8,128)}, f32[2,2,2,16,8,128]{5,4,3,2,1,0:T(8,128)}, u32[]{:S(2)}, u32[]{:S(2)}) collective-permute-start(f32[2,2,2,16,8,128]{5,4,3,2,1,0:T(8,128)} %get-tuple-element.24), channel_id=1, source_target_pairs={{0,96},{8,104},{16,112},{24,120},{32,0},{40,8},{48,16},{56,24},{64... | collective-permute-start | bytes 1572872 | tf_op jit(solution)/shard_map/ppermute | solution.py:120
  75.2 11.4 %copy-start = (f32[2,2,2,16,8,128]{5,4,3,2,1,0:T(8,128)}, f32[2,2,2,16,8,128]{5,4,3,2,1,0:T(8,128)S(1)}, u32[]{:S(2)}) copy-start(f32[2,2,2,16,8,128]{5,4,3,2,1,0:T(8,128)S(1)} %collective-permute-done.1.refs_3_.refs_1_) | copy-start | bytes 1572868
  89.4 16.2 %collective-permute-start.4 = (f32[4,2,16,8,128]{4,3,2,1,0:T(8,128)}, f32[4,2,16,8,128]{4,3,2,1,0:T(8,128)S(1)}, u32[]{:S(2)}, u32[]{:S(2)}) collective-permute-start(f32[4,2,16,8,128]{4,3,2,1,0:T(8,128)} %get-tuple-element.29), channel_id=1, source_target_pairs={{0,32},{8,40},{16,48},{24,56},{32,64},{40,72},{48,80},{56,88},{64,... | collective-permute-start | bytes 1572872 | tf_op jit(solution)/shard_map/ppermute | solution.py:120
  90.4 25.8 %collective-permute-start.5 = (f32[4,2,16,8,128]{4,3,2,1,0:T(8,128)}, f32[4,2,16,8,128]{4,3,2,1,0:T(8,128)}, u32[]{:S(2)}, u32[]{:S(2)}) collective-permute-start(f32[4,2,16,8,128]{4,3,2,1,0:T(8,128)} %get-tuple-element.30), channel_id=1, source_target_pairs={{0,64},{8,72},{16,80},{24,88},{32,96},{40,104},{48,112},{56,120},{... | collective-permute-start | bytes 1572872 | tf_op jit(solution)/shard_map/ppermute | solution.py:120
  92.8 23.5 %collective-permute-start.6 = (f32[4,2,16,8,128]{4,3,2,1,0:T(8,128)}, f32[4,2,16,8,128]{4,3,2,1,0:T(8,128)}, u32[]{:S(2)}, u32[]{:S(2)}) collective-permute-start(f32[4,2,16,8,128]{4,3,2,1,0:T(8,128)} %get-tuple-element.31), channel_id=1, source_target_pairs={{0,96},{8,104},{16,112},{24,120},{32,0},{40,8},{48,16},{56,24},{64... | collective-permute-start | bytes 1572872 | tf_op jit(solution)/shard_map/ppermute | solution.py:120
  94.7 23.8 %collective-permute-start.8 = (f32[4,2,16,8,128]{4,3,2,1,0:T(8,128)}, f32[4,2,16,8,128]{4,3,2,1,0:T(8,128)}, u32[]{:S(2)}, u32[]{:S(2)}) collective-permute-start(f32[4,2,16,8,128]{4,3,2,1,0:T(8,128)} %get-tuple-element.26.after_ref), channel_id=1, source_target_pairs={{0,16},{8,24},{16,0},{24,8},{32,48},{40,56},{48,32},{56,40},{64,80... | collective-permute-start | bytes 1572872 | tf_op jit(solution)/shard_map/ppermute | solution.py:120
  103.8 14.6 %collective-permute-start.9 = (f32[4,2,16,8,128]{4,3,2,1,0:T(8,128)}, f32[4,2,16,8,128]{4,3,2,1,0:T(8,128)}, u32[]{:S(2)}, u32[]{:S(2)}) collective-permute-start(f32[4,2,16,8,128]{4,3,2,1,0:T(8,128)} %get-tuple-element.32), channel_id=1, source_target_pairs={{0,24},{8,16},{16,8},{24,0},{32,56},{40,48},{48,40},{56,32},{64,88... | collective-permute-start | bytes 1572872 | tf_op jit(solution)/shard_map/ppermute | solution.py:120
  105.7 10.7 %copy-start.2 = (f32[4,2,16,8,128]{4,3,2,1,0:T(8,128)}, f32[4,2,16,8,128]{4,3,2,1,0:T(8,128)S(1)}, u32[]{:S(2)}) copy-start(f32[4,2,16,8,128]{4,3,2,1,0:T(8,128)S(1)} %collective-permute-done.4.refs_2_) | copy-start | bytes 1572868
  105.7 12.8 %collective-permute-start.10 = (f32[4,2,16,8,128]{4,3,2,1,0:T(8,128)}, f32[4,2,16,8,128]{4,3,2,1,0:T(8,128)}, u32[]{:S(2)}, u32[]{:S(2)}) collective-permute-start(f32[4,2,16,8,128]{4,3,2,1,0:T(8,128)} %shard_map.44), channel_id=1, source_target_pairs={{0,8},{8,0},{16,24},{24,16},{32,40},{40,32},{48,56},{56,48},{64,72... | collective-permute-start | bytes 1572872 | tf_op jit(solution)/shard_map/ppermute | solution.py:120
  127.6 5.4 %copy-start.1 = (f32[8,2,16,8,128]{4,3,2,1,0:T(8,128)S(1)}, f32[8,2,16,8,128]{4,3,2,1,0:T(8,128)}, u32[]{:S(2)}) copy-start(f32[8,2,16,8,128]{4,3,2,1,0:T(8,128)} %shard_map.42.refs_7_) | copy-start | bytes 3145732
  127.6 33.2 %all-to-all-start.2 = ((f32[16,256,128]{2,1,0:T(8,128)}), f32[16,256,128]{2,1,0:T(8,128)}, u32[]{:S(2)}, u32[]{:S(2)}) async-start(f32[16,256,128]{2,1,0:T(8,128)} %shard_map.45), calls=%async_computation.2 | async-start | bytes 4194304 | tf_op jit(solution)/shard_map/all_to_all | solution.py:417
  133.0 2.9 %collective-permute-start.7 = (f32[8,2,16,8,128]{4,3,2,1,0:T(8,128)S(1)}, f32[8,2,16,8,128]{4,3,2,1,0:T(8,128)}, u32[]{:S(2)}, u32[]{:S(2)}) collective-permute-start(f32[8,2,16,8,128]{4,3,2,1,0:T(8,128)S(1)} %copy-done.1), channel_id=1, source_target_pairs={{0,8},{8,0},{16,24},{24,16},{32,40},{40,32},{48,56},{56,48},{64,72... | collective-permute-start | bytes 3145736 | tf_op jit(solution)/shard_map/ppermute | solution.py:120
  160.8 32.7 %all-to-all-start.1 = ((f32[16,256,128]{2,1,0:T(8,128)}), f32[16,256,128]{2,1,0:T(8,128)}, u32[]{:S(2)}, u32[]{:S(2)}) async-start(f32[16,256,128]{2,1,0:T(8,128)} %shard_map.43), calls=%async_computation.1 | async-start | bytes 4194304 | tf_op jit(solution)/shard_map/all_to_all | solution.py:419

commit v6 on v5

--- a/solution.py
+++ b/solution.py
@@ -9,7 +9,7 @@
 from jax.sharding import PartitionSpec as P
 
 L = 16
-VMEM = 63 * 1024 * 1024
+VMEM = 64 * 1024 * 1024 - 384 * 1024
 F32 = jnp.float32
 BF16 = jnp.bfloat16
 BLOCK = (2, 16, 8, 128)

time: 200 us -> 200 us (level)
  no operation moved by 1% of the time
where the time goes in v6:
time: 200 us; the launch traced here: 196 us
  waiting for transfers between devices  101 us (50%)
  Pallas kernels  56 us (28%)
  starting transfers between devices  36.3 us (18%)
  local copies, waits for them, and re-layouts  2.7 us (1%)
    ppermute x11, waiting for transfers between devices, moved(): return lax.ppermute(values, 'mom', ways)  59.8 us
    all_to_all x1, waiting for transfers between devices, local(): near = lax.all_to_all(near, 'mom', 0, 0, tiled=True).reshape(16, *BLOCK)  25.2 us
    pallas_call x2, Pallas kernels, bubble_transform(): pl.pallas_call(functools.partial(bubble_body, h), grid=(8 // WIDE,), in_s...  18.1 us
    all_to_all x1, waiting for transfers between devices, local(): far = lax.all_to_all(far, 'mom', 0, 0, tiled=True).reshape(16, *BLOCK)  15.8 us
    ppermute x11, starting transfers between devices, moved(): return lax.ppermute(values, 'mom', ways)  15.3 us
    all_to_all x1, starting transfers between devices, local(): lax.all_to_all(greater_out.reshape(128, 64, 128), ('mom', 'tm'), 0, 0, ti...  10.7 us
    pallas_call x1, Pallas kernels, greater_transform(): pl.pallas_call(greater_body, grid=(2, steps), in_specs=[HBM, pl.BlockSpec...  8.58 us
    pallas_call x1, Pallas kernels, phase_tables(): pl.pallas_call(table_body, out_shape=(jax.ShapeDtypeStruct((512, 1024), B...  7.75 us
  transfers between devices with their start and end apart: 14, of which 7 were waited for; matrix products, arithmetic and copies ran while one was open for 1% of the time, Pallas kernels for 20%

profile of v6, /device:TPU:24, one launch (start us, length us, event | category | flops | bytes accessed | tf_op | source)
XLA Modules:
  0.0 196.2 jit_solution(6066214022234748541)
XLA Ops:
  0.0 5.4 %shard_map.37.after_ref = f32[4,4,8,8,8,128]{5,4,3,2,1,0:T(8,128)} custom-call(f32[2,16,4,32,256]{4,3,2,1,0:T(8,128)} %bitcast.11), custom_call_target="tpu_custom_call" | custom-call | flops 1 | bytes 1 | tf_op jit(solution)/shard_map/pallas_call | solution.py:270
  5.5 10.7 %all-to-all-start = ((f32[128,64,128]{2,1,0:T(8,128)}), f32[128,64,128]{2,1,0:T(8,128)}, u32[]{:S(2)}, u32[]{:S(2)}) async-start(f32[128,64,128]{2,1,0:T(8,128)} %bitcast.10), calls=%async_computation | async-start | bytes 8388608 | tf_op jit(solution)/shard_map/all_to_all | solution.py:408
  16.2 4.2 %shard_map.38 = (f32[4,2,2,16,8,128]{5,4,3,2,1,0:T(8,128)}, f32[4,2,2,16,8,128]{5,4,3,2,1,0:T(8,128)}, f32[2,2,2,16,8,128]{5,4,3,2,1,0:T(8,128)}, f32[2,2,2,16,8...) custom-call(s32[1]{0:T(128)} %bitcast.me_ref, ...), custom_call_target="tpu_custom_call" | custom-call | flops 1 | bytes 1 | tf_op jit(solution)/shard_map/pallas_call | solution.py:141
  20.4 1.8 collective-permute-start
  22.2 1.5 collective-permute-start.1
  23.7 2.7 %collective-permute-start.2 = (f32[2,2,2,16,8,128]{5,4,3,2,1,0:T(8,128)}, f32[2,2,2,16,8,128]{5,4,3,2,1,0:T(8,128)}, u32[]{:S(2)}, u32[]{:S(2)}) collective-permute-start(f32[2,2,2,16,8,128]{5,4,3,2,1,0:T(8,128)} %get-tuple-element.23), channel_id=1, source_target_pairs={{0,64},{8,72},{16,80},{24,88},{32,96},{40,104},{48,112},{56,120},{... | collective-permute-start | bytes 1572872 | tf_op jit(solution)/shard_map/ppermute | solution.py:120
  26.4 1.4 collective-permute-start.3
  28.0 0.7 reshape_reshape.6.lesser_ref
  28.7 0.9 reshape_reshape.8.result_ref
  29.8 0.7 reshape.35.greater_ref
  30.5 7.7 %shard_map.39 = (bf16[512,1024]{1,0:T(8,128)(2,1)}, bf16[512,1024]{1,0:T(8,128)(2,1)}, bf16[512,1024]{1,0:T(8,128)(2,1)}) custom-call(s32[1,512]{1,0:T(1,128)} %reshape_reshape.6.lesser_ref, s32[1,512]{1,0:T(1,128)} %reshape.35.greater_ref, s32[512,1]{1,0:T(8,128)} %reshape_reshape.8.result_ref), custom_call_target="tpu_custom_call" | custom-call | flops 1 | bytes 1 | tf_op jit(solution)/shard_map/pallas_call | solution.py:69
  38.3 37.0 %collective-permute-done.1.refs_3_.refs_1_ = f32[2,2,2,16,8,128]{5,4,3,2,1,0:T(8,128)} collective-permute-done((f32[2,2,2,16,8,128]{5,4,3,2,1,0:T(8,128)}, f32[2,2,2,16,8,128]{5,4,3,2,1,0:T(8,128)}, u32[]{:S(2)}, u32[]{:S(2)}) %collective-permute-start.1) | collective-permute-done | bytes 524320 | tf_op jit(solution)/shard_map/ppermute | solution.py:120
  75.3 11.3 %collective-permute-done.2.refs_4_.refs_2_ = f32[2,2,2,16,8,128]{5,4,3,2,1,0:T(8,128)} collective-permute-done((f32[2,2,2,16,8,128]{5,4,3,2,1,0:T(8,128)}, f32[2,2,2,16,8,128]{5,4,3,2,1,0:T(8,128)}, u32[]{:S(2)}, u32[]{:S(2)}) %collective-permute-start.2) | collective-permute-done | bytes 524320 | tf_op jit(solution)/shard_map/ppermute | solution.py:120
  86.6 2.8 %shard_map.40 = (f32[4,2,16,8,128]{4,3,2,1,0:T(8,128)}, f32[4,2,16,8,128]{4,3,2,1,0:T(8,128)}, f32[4,2,16,8,128]{4,3,2,1,0:T(8,128)}, f32[4,2,16,8,128]{4,3,2,1,0:T(8,128)}, f32[4,2,16,8,128]{4,3,2,1,0:T(8,128)}) custom-call(f32[4,2,2,16,8,128]{5,4,3,2,1,0:T(8,128)} %get-tuple-element.19.refs_0_, f32[4,2,2,16,8,128]{5,4,3,2,1,0:T(8,128)} %collective-permute-done.refs_1_, ...), custom_call_target="tpu_custom_call" | custom-call | flops 1 | bytes 1 | tf_op jit(solution)/shard_map/pallas_call | solution.py:169
  89.4 1.0 collective-permute-start.4
  90.4 2.4 %collective-permute-start.5 = (f32[4,2,16,8,128]{4,3,2,1,0:T(8,128)}, f32[4,2,16,8,128]{4,3,2,1,0:T(8,128)}, u32[]{:S(2)}, u32[]{:S(2)}) collective-permute-start(f32[4,2,16,8,128]{4,3,2,1,0:T(8,128)} %get-tuple-element.30), channel_id=1, source_target_pairs={{0,64},{8,72},{16,80},{24,88},{32,96},{40,104},{48,112},{56,120},{... | collective-permute-start | bytes 1572872 | tf_op jit(solution)/shard_map/ppermute | solution.py:120
  92.8 1.9 collective-permute-start.6
  94.7 0.6 collective-permute-start.8
  95.2 8.6 %shard_map.41.refs_5_.g_ref.refs_4_ = f32[2,2,512,512]{3,2,1,0:T(8,128)} custom-call(f32[4,2,16,8,128]{4,3,2,1,0:T(8,128)} %get-tuple-element.26.after_ref, f32[16,8,8,8,128]{4,3,2,1,0:T(8,128)} %bitcast.5.x_ref, bf16[512,1024]{1,0:T(8,128)(2,1)} %get-tuple-element.27.table_ref), custom_call_target="tpu_custom_call" | custom-call | flops 1 | bytes 1 | tf_op jit(solution)/shard_map/pallas_call | solution.py:314
  103.8 1.8 shard_map.44
  105.7 1.6 collective-permute-start.10
  107.3 9.0 %collective-permute-done.5.refs_3_ = f32[4,2,16,8,128]{4,3,2,1,0:T(8,128)} collective-permute-done((f32[4,2,16,8,128]{4,3,2,1,0:T(8,128)}, f32[4,2,16,8,128]{4,3,2,1,0:T(8,128)}, u32[]{:S(2)}, u32[]{:S(2)}) %collective-permute-start.5) | collective-permute-done | bytes 524320 | tf_op jit(solution)/shard_map/ppermute | solution.py:120
  116.3 2.1 %shard_map.42.refs_7_ = f32[8,2,16,8,128]{4,3,2,1,0:T(8,128)} custom-call(f32[4,2,2,16,8,128]{5,4,3,2,1,0:T(8,128)} %get-tuple-element.19.refs_0_, f32[4,2,2,16,8,128]{5,4,3,2,1,0:T(8,128)} %collective-permute-done.refs_1_, f32[4,2,16,8,128]{4,3,2,1,0:T(8,128)} %collective-permute-done.4.refs_2_, f32[4,2,16,8,128]{4,3,2,1,0:T(8,128)} %collective-permute-done.5.refs_3_, ...), custom_call_target="tpu_custom_call" | custom-call | flops 1 | bytes 1 | tf_op jit(solution)/shard_map/pallas_call | solution.py:169
  118.5 9.1 %shard_map.45 = f32[16,256,128]{2,1,0:T(8,128)} custom-call(s32[1]{0:T(128)} %bitcast.me_ref, f32[2,2,512,512]{3,2,1,0:T(8,128)} %shard_map.41.refs_5_.g_ref.refs_4_, bf16[512,1024]{1,0:T(8,128)(2,1)} %get-tuple-element.25.refs_6_.forward_hbm, bf16[512,1024]{1,0:T(8,128)(2,1)} %get-tuple-element.28.backward_hbm, ...), custom_call_target="tpu_custom_call" | custom-call | flops 1 | bytes 1 | tf_op jit(solution)/shard_map/pallas_call | solution.py:381
  127.6 5.4 %all-to-all-start.2 = ((f32[16,256,128]{2,1,0:T(8,128)}), f32[16,256,128]{2,1,0:T(8,128)}, u32[]{:S(2)}, u32[]{:S(2)}) async-start(f32[16,256,128]{2,1,0:T(8,128)} %shard_map.45), calls=%async_computation.2 | async-start | bytes 4194304 | tf_op jit(solution)/shard_map/all_to_all | solution.py:417
  133.4 2.4 %collective-permute-done.7.refs_5_ = f32[8,2,16,8,128]{4,3,2,1,0:T(8,128)} collective-permute-done((f32[8,2,16,8,128]{4,3,2,1,0:T(8,128)S(1)}, f32[8,2,16,8,128]{4,3,2,1,0:T(8,128)}, u32[]{:S(2)}, u32[]{:S(2)}) %collective-permute-start.7) | collective-permute-done | bytes 1048608 | tf_op jit(solution)/shard_map/ppermute | solution.py:120
  135.8 9.1 %shard_map.43 = f32[16,256,128]{2,1,0:T(8,128)} custom-call(s32[1]{0:T(128)} %bitcast.me_ref, f32[2,2,512,512]{3,2,1,0:T(8,128)} %shard_map.41.refs_5_.g_ref.refs_4_, bf16[512,1024]{1,0:T(8,128)(2,1)} %get-tuple-element.25.refs_6_.forward_hbm, bf16[512,1024]{1,0:T(8,128)(2,1)} %get-tuple-element.28.backward_hbm, ...), custom_call_target="tpu_custom_call" | custom-call | flops 1 | bytes 1 | tf_op jit(solution)/shard_map/pallas_call | solution.py:381
  144.9 15.8 %all-to-all-done.2 = f32[16,256,128]{2,1,0:T(8,128)} async-done(((f32[16,256,128]{2,1,0:T(8,128)}), f32[16,256,128]{2,1,0:T(8,128)}, u32[]{:S(2)}, u32[]{:S(2)}) %all-to-all-start.2) | async-done | bytes 2097184 | tf_op jit(solution)/shard_map/all_to_all | solution.py:417
  160.8 4.9 %all-to-all-start.1 = ((f32[16,256,128]{2,1,0:T(8,128)}), f32[16,256,128]{2,1,0:T(8,128)}, u32[]{:S(2)}, u32[]{:S(2)}) async-start(f32[16,256,128]{2,1,0:T(8,128)} %shard_map.43), calls=%async_computation.1 | async-start | bytes 4194304 | tf_op jit(solution)/shard_map/all_to_all | solution.py:419
  165.7 2.6 %shard_map.46.refs_1_ = f32[2,16,4,32,256]{4,3,2,1,0:T(8,128)} custom-call(f32[16,2,16,8,128]{4,3,2,1,0:T(8,128)} %bitcast.7.refs_0_), custom_call_target="tpu_custom_call" | custom-call | flops 1 | bytes 1 | tf_op jit(solution)/shard_map/pallas_call | solution.py:227
  168.2 25.2 %all-to-all-done.1 = f32[16,256,128]{2,1,0:T(8,128)} async-done(((f32[16,256,128]{2,1,0:T(8,128)}), f32[16,256,128]{2,1,0:T(8,128)}, u32[]{:S(2)}, u32[]{:S(2)}) %all-to-all-start.1) | async-done | bytes 2097184 | tf_op jit(solution)/shard_map/all_to_all | solution.py:419
  193.4 2.6 %shard_map.47 = f32[2,16,4,32,256]{4,3,2,1,0:T(8,128)} custom-call(f32[16,2,16,8,128]{4,3,2,1,0:T(8,128)} %bitcast.6.refs_0_, f32[2,16,4,32,256]{4,3,2,1,0:T(8,128)} %shard_map.46.refs_1_), custom_call_target="tpu_custom_call", output_to_operand_aliasing={{}: (1, {})} | custom-call | flops 1 | bytes 1 | tf_op jit(solution)/shard_map/pallas_call | solution.py:227
  (19 shorter events, 1.0 us)
Async XLA Ops:
  5.5 89.8 %all-to-all-start = ((f32[128,64,128]{2,1,0:T(8,128)}), f32[128,64,128]{2,1,0:T(8,128)}, u32[]{:S(2)}, u32[]{:S(2)}) async-start(f32[128,64,128]{2,1,0:T(8,128)} %bitcast.10), calls=%async_computation | async-start | bytes 8388608 | tf_op jit(solution)/shard_map/all_to_all | solution.py:408
  16.2 11.6 %copy-start.1 = (s32[256]{0:T(256)S(1)}, s32[256]{0:T(256)}, u32[]{:S(2)}) copy-start(s32[256]{0:T(256)} %param.5) | copy-start | bytes 3076
  20.4 66.2 %collective-permute-start = (f32[4,2,2,16,8,128]{5,4,3,2,1,0:T(8,128)}, f32[4,2,2,16,8,128]{5,4,3,2,1,0:T(8,128)}, u32[]{:S(2)}, u32[]{:S(2)}) collective-permute-start(f32[4,2,2,16,8,128]{5,4,3,2,1,0:T(8,128)} %get-tuple-element.20), channel_id=1, source_target_pairs={{0,16},{8,24},{16,0},{24,8},{32,48},{40,56},{48,32},{56,40},{64,80... | collective-permute-start | bytes 3145736 | tf_op jit(solution)/shard_map/ppermute | solution.py:120
  22.2 53.1 %collective-permute-start.1 = (f32[2,2,2,16,8,128]{5,4,3,2,1,0:T(8,128)}, f32[2,2,2,16,8,128]{5,4,3,2,1,0:T(8,128)}, u32[]{:S(2)}, u32[]{:S(2)}) collective-permute-start(f32[2,2,2,16,8,128]{5,4,3,2,1,0:T(8,128)} %get-tuple-element.22), channel_id=1, source_target_pairs={{0,32},{8,40},{16,48},{24,56},{32,64},{40,72},{48,80},{56,88},{64,... | collective-permute-start | bytes 1572872 | tf_op jit(solution)/shard_map/ppermute | solution.py:120
  23.7 62.9 %collective-permute-start.2 = (f32[2,2,2,16,8,128]{5,4,3,2,1,0:T(8,128)}, f32[2,2,2,16,8,128]{5,4,3,2,1,0:T(8,128)}, u32[]{:S(2)}, u32[]{:S(2)}) collective-permute-start(f32[2,2,2,16,8,128]{5,4,3,2,1,0:T(8,128)} %get-tuple-element.23), channel_id=1, source_target_pairs={{0,64},{8,72},{16,80},{24,88},{32,96},{40,104},{48,112},{56,120},{... | collective-permute-start | bytes 1572872 | tf_op jit(solution)/shard_map/ppermute | solution.py:120
  26.4 60.2 %collective-permute-start.3 = (f32[2,2,2,16,8,128]{5,4,3,2,1,0:T(8,128)}, f32[2,2,2,16,8,128]{5,4,3,2,1,0:T(8,128)}, u32[]{:S(2)}, u32[]{:S(2)}) collective-permute-start(f32[2,2,2,16,8,128]{5,4,3,2,1,0:T(8,128)} %get-tuple-element.24), channel_id=1, source_target_pairs={{0,96},{8,104},{16,112},{24,120},{32,0},{40,8},{48,16},{56,24},{64... | collective-permute-start | bytes 1572872 | tf_op jit(solution)/shard_map/ppermute | solution.py:120
  89.4 16.2 %collective-permute-start.4 = (f32[4,2,16,8,128]{4,3,2,1,0:T(8,128)}, f32[4,2,16,8,128]{4,3,2,1,0:T(8,128)}, u32[]{:S(2)}, u32[]{:S(2)}) collective-permute-start(f32[4,2,16,8,128]{4,3,2,1,0:T(8,128)} %get-tuple-element.29), channel_id=1, source_target_pairs={{0,32},{8,40},{16,48},{24,56},{32,64},{40,72},{48,80},{56,88},{64,... | collective-permute-start | bytes 1572872 | tf_op jit(solution)/shard_map/ppermute | solution.py:120
  90.4 25.8 %collective-permute-start.5 = (f32[4,2,16,8,128]{4,3,2,1,0:T(8,128)}, f32[4,2,16,8,128]{4,3,2,1,0:T(8,128)}, u32[]{:S(2)}, u32[]{:S(2)}) collective-permute-start(f32[4,2,16,8,128]{4,3,2,1,0:T(8,128)} %get-tuple-element.30), channel_id=1, source_target_pairs={{0,64},{8,72},{16,80},{24,88},{32,96},{40,104},{48,112},{56,120},{... | collective-permute-start | bytes 1572872 | tf_op jit(solution)/shard_map/ppermute | solution.py:120
  92.8 23.5 %collective-permute-start.6 = (f32[4,2,16,8,128]{4,3,2,1,0:T(8,128)}, f32[4,2,16,8,128]{4,3,2,1,0:T(8,128)}, u32[]{:S(2)}, u32[]{:S(2)}) collective-permute-start(f32[4,2,16,8,128]{4,3,2,1,0:T(8,128)} %get-tuple-element.31), channel_id=1, source_target_pairs={{0,96},{8,104},{16,112},{24,120},{32,0},{40,8},{48,16},{56,24},{64... | collective-permute-start | bytes 1572872 | tf_op jit(solution)/shard_map/ppermute | solution.py:120
  94.7 23.8 %collective-permute-start.8 = (f32[4,2,16,8,128]{4,3,2,1,0:T(8,128)}, f32[4,2,16,8,128]{4,3,2,1,0:T(8,128)}, u32[]{:S(2)}, u32[]{:S(2)}) collective-permute-start(f32[4,2,16,8,128]{4,3,2,1,0:T(8,128)} %get-tuple-element.26.after_ref), channel_id=1, source_target_pairs={{0,16},{8,24},{16,0},{24,8},{32,48},{40,56},{48,32},{56,40},{64,80... | collective-permute-start | bytes 1572872 | tf_op jit(solution)/shard_map/ppermute | solution.py:120
  103.8 14.6 %collective-permute-start.9 = (f32[4,2,16,8,128]{4,3,2,1,0:T(8,128)}, f32[4,2,16,8,128]{4,3,2,1,0:T(8,128)}, u32[]{:S(2)}, u32[]{:S(2)}) collective-permute-start(f32[4,2,16,8,128]{4,3,2,1,0:T(8,128)} %get-tuple-element.32), channel_id=1, source_target_pairs={{0,24},{8,16},{16,8},{24,0},{32,56},{40,48},{48,40},{56,32},{64,88... | collective-permute-start | bytes 1572872 | tf_op jit(solution)/shard_map/ppermute | solution.py:120
  105.7 12.8 %collective-permute-start.10 = (f32[4,2,16,8,128]{4,3,2,1,0:T(8,128)}, f32[4,2,16,8,128]{4,3,2,1,0:T(8,128)}, u32[]{:S(2)}, u32[]{:S(2)}) collective-permute-start(f32[4,2,16,8,128]{4,3,2,1,0:T(8,128)} %shard_map.44), channel_id=1, source_target_pairs={{0,8},{8,0},{16,24},{24,16},{32,40},{40,32},{48,56},{56,48},{64,72... | collective-permute-start | bytes 1572872 | tf_op jit(solution)/shard_map/ppermute | solution.py:120
  127.6 5.4 %copy-start = (f32[8,2,16,8,128]{4,3,2,1,0:T(8,128)S(1)}, f32[8,2,16,8,128]{4,3,2,1,0:T(8,128)}, u32[]{:S(2)}) copy-start(f32[8,2,16,8,128]{4,3,2,1,0:T(8,128)} %shard_map.42.refs_7_) | copy-start | bytes 3145732
  127.6 33.2 %all-to-all-start.2 = ((f32[16,256,128]{2,1,0:T(8,128)}), f32[16,256,128]{2,1,0:T(8,128)}, u32[]{:S(2)}, u32[]{:S(2)}) async-start(f32[16,256,128]{2,1,0:T(8,128)} %shard_map.45), calls=%async_computation.2 | async-start | bytes 4194304 | tf_op jit(solution)/shard_map/all_to_all | solution.py:417
  133.0 2.9 %collective-permute-start.7 = (f32[8,2,16,8,128]{4,3,2,1,0:T(8,128)S(1)}, f32[8,2,16,8,128]{4,3,2,1,0:T(8,128)}, u32[]{:S(2)}, u32[]{:S(2)}) collective-permute-start(f32[8,2,16,8,128]{4,3,2,1,0:T(8,128)S(1)} %copy-done), channel_id=1, source_target_pairs={{0,8},{8,0},{16,24},{24,16},{32,40},{40,32},{48,56},{56,48},{64,72... | collective-permute-start | bytes 3145736 | tf_op jit(solution)/shard_map/ppermute | solution.py:120
  160.8 32.7 %all-to-all-start.1 = ((f32[16,256,128]{2,1,0:T(8,128)}), f32[16,256,128]{2,1,0:T(8,128)}, u32[]{:S(2)}, u32[]{:S(2)}) async-start(f32[16,256,128]{2,1,0:T(8,128)} %shard_map.43), calls=%async_computation.1 | async-start | bytes 4194304 | tf_op jit(solution)/shard_map/all_to_all | solution.py:419
